TPU v7x, 32 devices: a whole 2x2x4 slice. The times are simulated.
32 devices in a mesh: group: 2 (over y), region: 4 (over z), hid: 2 (over x), sub: 2 (over core).
Axes of the slice: x: 2, y: 2, z: 4, core: 2. Of those that a mesh axis runs over, the one named last changes fastest.
Arguments:
- edge_lat: bfloat16 [40960, 512], P(('group', 'region', 'sub')), parts along dimension 0, may hold values from -6 to 6
- node_lat: bfloat16 [4096, 512], P(('group', 'region', 'sub')), parts along dimension 0, may hold values from -6 to 6
- senders: int32 [40960], P(('group', 'region', 'sub')), parts along dimension 0, may hold values from 0 to 511
- recv_slots: int32 [40960], P(('group', 'region', 'sub')), parts along dimension 0, may hold values from 0 to 127
- owners: int32 [320, 1], P(('group', 'region', 'sub')), parts along dimension 0, may hold values from 0 to 3; in each aligned block of 20 rows (0 to 19, 20 to 39, ...) at most 7 rows name the same one
- targets: int32 [320], P(('group', 'region', 'sub')), parts along dimension 0, may hold values from 0 to 1
- w_edge_in: bfloat16 [1024, 512], P(None, 'hid'), may hold values from -0.1875 to 0.1875
- b_edge: bfloat16 [512], P('hid'), may hold values from -3 to 3
- w_edge_out: bfloat16 [512, 512], P('hid'), may hold values from -0.25 to 0.25
- w_node_in: bfloat16 [1024, 512], P(None, 'hid'), may hold values from -0.1875 to 0.1875
- b_node: bfloat16 [512], P('hid'), may hold values from -3 to 3
- w_node_out: bfloat16 [512, 512], P('hid'), may hold values from -0.25 to 0.25
- norm_gain: bfloat16 [512], replicated, may hold values from 0.099609375 to 1.8984375
- cotangent: bfloat16 [4096, 512], P(('group', 'region', 'sub')), parts along dimension 0, may hold values from -6 to 6
Outputs:
- new_nodes: bfloat16 [4096, 512], P(('group', 'region', 'sub')), parts along dimension 0
- grad_nodes: bfloat16 [4096, 512], P(('group', 'region', 'sub')), parts along dimension 0
- grad_edge_in: float32 [2048, 512], P('group', 'hid'), parts along dimension 0
- grad_edge_out: float32 [1024, 512], P(('group', 'hid')), parts along dimension 0
- grad_node_in: float32 [2048, 512], P('group', 'hid'), parts along dimension 0
- grad_node_out: float32 [1024, 512], P(('group', 'hid')), parts along dimension 0
There are 2 independent parts, one for each index of `group`. A program takes and returns all parts, laid end to end along the dimension named above; an argument that names none is the same for every part. Nothing has to cross between parts.
Inputs may be any that keep to these rules, and one draw needn't show every extreme that they name: `owners`: among the 20 blocks of one index of region and sub, no region is named by more than 7 blocks, a bound that some block reaches of them in every draw.
All inputs are finite; a program needn't handle non-finite values.
Results may differ from a plain program's by a relative error of at most 0.023.
Values may be sent and summed in bfloat16 or wider, within the bound.
A program may use at most 128 MiB of HBM per device.

v0:
```python
import jax
import jax.numpy as jnp
from jax import lax
from jax.sharding import PartitionSpec as P


def silu_slope(values):
    logistic = jax.nn.sigmoid(values)
    return logistic * (1.0 + values * (1.0 - logistic))


def layer_norm(values, norm_gain):
    row_mean = jnp.mean(values, axis=-1, keepdims=True)
    centred = values - row_mean
    spread = jnp.mean(centred * centred, axis=-1, keepdims=True)
    return centred * lax.rsqrt(spread + 1e-05) * norm_gain


def edge_forward(
    lat_rows, send_ids, slot_ids, region_nodes, weight_in, bias, block_count, block_rows
):
    inputs = jnp.concatenate([lat_rows, jnp.take(region_nodes, send_ids, axis=0)], axis=1)
    edge_pre = jnp.dot(inputs, weight_in, preferred_element_type=jnp.float32) + bias.astype(
        jnp.float32
    )
    hidden = jax.nn.silu(edge_pre).astype(jnp.bfloat16)
    width = hidden.shape[1]
    positions = jnp.arange(block_rows, dtype=jnp.int32)
    onehot = (
        slot_ids.reshape(block_count, block_rows)[:, :, None] == positions[None, None, :]
    ).astype(jnp.bfloat16)
    summed = jnp.einsum(
        "beq,beh->bqh",
        onehot,
        hidden.reshape(block_count, block_rows, width),
        preferred_element_type=jnp.float32,
    ).astype(jnp.bfloat16)
    return (inputs, edge_pre, onehot, summed)


def edge_backward(grad_rows, inputs, edge_pre, onehot, summed, weight_in, weight_out, latent):
    width = summed.shape[2]
    grad_summed = jnp.einsum(
        "bql,hl->bqh", grad_rows, weight_out, preferred_element_type=jnp.float32
    ).astype(jnp.bfloat16)
    grad_out = jnp.einsum("bqh,bql->hl", summed, grad_rows, preferred_element_type=jnp.float32)
    grad_hidden = jnp.einsum(
        "beq,bqh->beh", onehot, grad_summed, preferred_element_type=jnp.float32
    ).reshape(-1, width)
    grad_pre = (grad_hidden * silu_slope(edge_pre)).astype(jnp.bfloat16)
    grad_in = jnp.einsum("ei,eh->ih", inputs, grad_pre, preferred_element_type=jnp.float32)
    grad_send = jnp.einsum(
        "eh,lh->el", grad_pre, weight_in[latent:], preferred_element_type=jnp.float32
    )
    return (grad_in, grad_out, grad_send)


def into_slots(values, source, filled, regions, capacity):
    picked = jnp.take(values, source, axis=0)
    picked = jnp.where(filled[:, None, None], picked, jnp.zeros((), values.dtype))
    return picked.reshape((regions, capacity) + values.shape[1:])


def on_device(
    edge_lat,
    node_lat,
    senders,
    recv_slots,
    owners,
    targets,
    w_edge_in,
    b_edge,
    w_edge_out,
    w_node_in,
    b_node,
    w_node_out,
    norm_gain,
    cotangent,
):
    regions = lax.axis_size("region")
    sub_index = lax.axis_index("sub")
    blocks = owners.shape[0]
    block_rows = recv_slots.shape[0] // blocks
    node_rows = node_lat.shape[0]
    latent = node_lat.shape[1]
    recv_blocks = node_rows // block_rows
    capacity = max(2, (5 * blocks + 4 * regions - 1) // (4 * regions))
    region_nodes = lax.all_gather(node_lat, "sub", axis=0, tiled=True)
    block_owner = owners[:, 0]
    block_order = jnp.arange(blocks, dtype=jnp.int32)
    earlier = (block_owner[None, :] == block_owner[:, None]) & (
        block_order[None, :] < block_order[:, None]
    )
    block_rank = jnp.sum(earlier.astype(jnp.int32), axis=1)
    slot_of_block = block_owner * capacity + block_rank
    places = jnp.arange(regions * capacity, dtype=jnp.int32)
    slot_match = slot_of_block[None, :] == places[:, None]
    filled = jnp.any(slot_match, axis=1)
    source = jnp.sum(jnp.where(slot_match, block_order[None, :], 0), axis=1)
    out_targets = jnp.where(filled, jnp.take(targets, source), 0).reshape(regions, capacity)
    target_codes = jnp.arange(recv_blocks, dtype=jnp.int32)
    edge_in_w, edge_out_w = (w_edge_in, w_edge_out)
    inputs, edge_pre, onehot, summed = edge_forward(
        edge_lat, senders, recv_slots, region_nodes, w_edge_in, b_edge, blocks, block_rows
    )
    messages = jnp.einsum(
        "bqh,hl->bql", summed, w_edge_out, preferred_element_type=jnp.float32
    ).astype(jnp.bfloat16)
    outgoing = into_slots(messages, source, filled, regions, capacity)
    arrived, in_targets = (
        lax.all_to_all(outgoing, "region", split_axis=0, concat_axis=0, tiled=True),
        lax.all_to_all(out_targets, "region", split_axis=0, concat_axis=0, tiled=True),
    )
    target_pick = (in_targets.reshape(-1)[:, None] == target_codes[None, :]).astype(jnp.bfloat16)
    partial_agg = jnp.einsum(
        "sr,sql->rql",
        target_pick,
        arrived.reshape(-1, block_rows, latent),
        preferred_element_type=jnp.float32,
    )
    gathered = lax.psum(partial_agg.reshape(node_rows, latent).astype(jnp.bfloat16), "hid")
    node_in = jnp.concatenate([node_lat, gathered], axis=1)
    node_pre = jnp.dot(node_in, w_node_in, preferred_element_type=jnp.float32) + b_node.astype(
        jnp.float32
    )
    node_hidden = jax.nn.silu(node_pre).astype(jnp.bfloat16)
    update = lax.psum(
        jnp.dot(node_hidden, w_node_out, preferred_element_type=jnp.float32).astype(jnp.bfloat16),
        "hid",
    ).astype(jnp.float32)
    gain_values = norm_gain.astype(jnp.float32)
    normed, norm_back = jax.vjp(lambda values: layer_norm(values, gain_values), update)
    new_nodes = (node_lat.astype(jnp.float32) + normed).astype(jnp.bfloat16)
    grad_update = norm_back(cotangent.astype(jnp.float32))[0].astype(jnp.bfloat16)
    grad_node_out = jnp.einsum(
        "nh,nl->hl", node_hidden, grad_update, preferred_element_type=jnp.float32
    )
    grad_node_pre = (
        jnp.einsum("nl,hl->nh", grad_update, w_node_out, preferred_element_type=jnp.float32)
        * silu_slope(node_pre)
    ).astype(jnp.bfloat16)
    grad_node_in = jnp.einsum(
        "ni,nh->ih", node_in, grad_node_pre, preferred_element_type=jnp.float32
    )
    grad_node_cat = jnp.einsum(
        "nh,ih->ni", grad_node_pre, w_node_in, preferred_element_type=jnp.float32
    )
    grad_gathered = lax.psum(grad_node_cat[:, latent:].astype(jnp.bfloat16), "hid")
    replies = jnp.take(
        grad_gathered.reshape(recv_blocks, block_rows, latent), in_targets.reshape(-1), axis=0
    )
    replies = replies.reshape(regions, capacity, block_rows, latent)
    returned = lax.all_to_all(replies, "region", split_axis=0, concat_axis=0, tiled=True)
    grad_rows = jnp.take(
        returned.reshape(regions * capacity, block_rows, latent), slot_of_block, axis=0
    )
    grad_edge_in, grad_edge_out, grad_send = edge_backward(
        grad_rows, inputs, edge_pre, onehot, summed, edge_in_w, edge_out_w, latent
    )
    sender_part = jax.ops.segment_sum(grad_send, senders, num_segments=region_nodes.shape[0])
    own_grads = (
        lax.dynamic_slice_in_dim(sender_part, sub_index * node_rows, node_rows, 0)
        + grad_node_cat[:, :latent]
    )
    sender_part = lax.dynamic_update_slice_in_dim(sender_part, own_grads, sub_index * node_rows, 0)
    summed_grads = lax.psum(sender_part.astype(jnp.bfloat16), ("hid", "sub")).astype(jnp.float32)
    grad_nodes = (
        cotangent.astype(jnp.float32)
        + lax.dynamic_slice_in_dim(summed_grads, sub_index * node_rows, node_rows, 0)
    ).astype(jnp.bfloat16)
    grad_edge_in, grad_edge_out, grad_node_in, grad_node_out = (
        lax.psum(grad_edge_in.astype(jnp.bfloat16), ("region", "sub")).astype(jnp.float32),
        lax.psum(grad_edge_out.astype(jnp.bfloat16), ("region", "sub")).astype(jnp.float32),
        lax.psum(grad_node_in.astype(jnp.bfloat16), ("region", "sub")).astype(jnp.float32),
        lax.psum(grad_node_out.astype(jnp.bfloat16), ("region", "sub")).astype(jnp.float32),
    )
    return (new_nodes, grad_nodes, grad_edge_in, grad_edge_out, grad_node_in, grad_node_out)


def solution(mesh):
    placed = (
        P(("group", "region", "sub"), None),
        P(("group", "region", "sub"), None),
        P(("group", "region", "sub")),
        P(("group", "region", "sub")),
        P(("group", "region", "sub"), None),
        P(("group", "region", "sub")),
        P(None, "hid"),
        P("hid"),
        P("hid", None),
        P(None, "hid"),
        P("hid"),
        P("hid", None),
        P(),
        P(("group", "region", "sub"), None),
    )
    return jax.shard_map(
        on_device,
        mesh=mesh,
        in_specs=placed,
        out_specs=(
            P(("group", "region", "sub"), None),
            P(("group", "region", "sub"), None),
            P("group", "hid"),
            P(("group", "hid"), None),
            P("group", "hid"),
            P(("group", "hid"), None),
        ),
        check_vma=False,
    )
```

profile of v0, /device:TPU:25, one launch (start us, length us, event | category | flops | bytes accessed | tf_op | source)
XLA Modules:
  0.0 454.1 jit_solution(16824067294823182922)
XLA Ops:
  7.2 0.9 convert_reduce_fusion.1
  8.1 0.7 multiply_add_fusion.1
  8.8 0.1 select_reduce_fusion
  8.8 0.1 fusion.33
  9.0 1.4 gather_fusion
  10.5 0.1 reduce_or.12
  10.6 0.6 select_select_fusion.1
  11.2 4.5 all-to-all-start
  15.7 0.7 compare_select_fusion
  16.4 0.7 compare_and_fusion
  17.2 0.1 broadcast_in_dim.97
  17.3 3.2 all_gather.3
  20.5 0.7 convert_element_type.96
  21.2 8.2 %gather_fusion.1 = bf16[2560,512]{1,0:T(8,128)(2,1)} fusion(bf16[512,512]{1,0:T(8,128)(2,1)S(1)} %all_gather.3, s32[3072]{0:T(1024)S(1)} %pad_clamp_fusion), kind=kCustom, calls=%fused_computation.1 | custom fusion | bytes 5253120 | tf_op jit(solution)/shard_map/jit(_take)/gather | solution.py:22
  29.4 2.8 broadcast_select_fusion.2
  32.2 2.8 multiply_convert_fusion
  35.1 1.2 convolution_convert_fusion.2
  36.3 1.1 copy-done.1
  37.3 0.8 convolution_convert_fusion
  38.2 2.7 gather_fusion.2
  40.9 4.3 select_select_fusion
  45.2 4.8 %all-to-all-start.1 = ((bf16[4,7,128,512]{3,2,1,0:T(8,128)(2,1)}), bf16[4,7,128,512]{3,2,1,0:T(8,128)(2,1)}, u32[]{:S(2)}, u32[]{:S(2)}) async-start(bf16[4,7,128,512]{3,2,1,0:T(8,128)(2,1)} %select_select_fusion), calls=%async_computation.1 | async-start | bytes 7340032 | tf_op jit(solution)/shard_map/all_to_all | solution.py:111
  50.0 0.5 broadcast.244
  50.5 0.7 reduce.5
  51.1 0.1 eq.64
  51.2 78.2 %all-to-all-done.1 = bf16[4,7,128,512]{3,2,1,0:T(8,128)(2,1)} async-done(((bf16[4,7,128,512]{3,2,1,0:T(8,128)(2,1)}), bf16[4,7,128,512]{3,2,1,0:T(8,128)(2,1)}, u32[]{:S(2)}, u32[]{:S(2)}) %all-to-all-start.1) | async-done | bytes 3670048 | tf_op jit(solution)/shard_map/all_to_all | solution.py:111
  129.5 4.3 fusion.7
  133.8 0.7 copy.35
  134.6 24.4 %all-reduce.7.cloned.1.call-done = bf16[256,512]{1,0:T(8,128)(2,1)} async-done(((bf16[256,512]{1,0:T(8,128)(2,1)}), bf16[256,512]{1,0:T(8,128)(2,1)}) %all-reduce.7.cloned.1.call-update) | async-done | bytes 262160 | tf_op jit(solution)/shard_map/psum | solution.py:121
  159.0 1.0 constant_dynamic-update-slice_fusion
  160.0 0.3 convolution_add_fusion.1
  160.3 0.9 convolution_convert_fusion.5
  161.5 23.7 %all-reduce.9.cloned.1.call-done = bf16[256,512]{1,0:T(8,128)(2,1)} async-done(((bf16[256,512]{1,0:T(8,128)(2,1)}), bf16[256,512]{1,0:T(8,128)(2,1)}) %all-reduce.9.cloned.1.call-update) | async-done | bytes 262160 | tf_op jit(solution)/shard_map/psum | solution.py:127
  185.2 1.1 convert_reduce_fusion
  186.3 1.2 fusion.22
  187.5 1.2 fusion.27
  188.8 1.9 add_convert_fusion
  190.7 0.3 fusion.10
  191.0 0.3 fusion.47
  191.3 0.8 slice.31
  192.2 23.3 %all-reduce.11.cloned.1.call-done = bf16[2,128,512]{2,1,0:T(8,128)(2,1)} async-done(((bf16[2,128,512]{2,1,0:T(8,128)(2,1)}), bf16[2,128,512]{2,1,0:T(8,128)(2,1)}) %all-reduce.11.cloned.1.call-update) | async-done | bytes 262160 | tf_op jit(solution)/shard_map/psum | solution.py:148
  215.5 3.6 gather_fusion.3
  219.1 4.3 broadcast_select_fusion
  223.4 5.1 %all-to-all-start.2 = ((bf16[4,7,128,512]{3,2,1,0:T(8,128)(2,1)}), bf16[4,7,128,512]{3,2,1,0:T(8,128)(2,1)}, u32[]{:S(2)}, u32[]{:S(2)}) async-start(bf16[4,7,128,512]{3,2,1,0:T(8,128)(2,1)} %broadcast_select_fusion), calls=%async_computation.2 | async-start | bytes 7340032 | tf_op jit(solution)/shard_map/all_to_all | solution.py:153
  228.5 1.0 convolution_convert_fusion.4
  229.5 1.1 convolution_convert_fusion.3
  230.7 76.6 %all-to-all-done.2 = bf16[4,7,128,512]{3,2,1,0:T(8,128)(2,1)} async-done(((bf16[4,7,128,512]{3,2,1,0:T(8,128)(2,1)}), bf16[4,7,128,512]{3,2,1,0:T(8,128)(2,1)}, u32[]{:S(2)}, u32[]{:S(2)}) %all-to-all-start.2) | async-done | bytes 3670048 | tf_op jit(solution)/shard_map/all_to_all | solution.py:153
  307.3 4.4 gather_fusion.4
  311.7 4.7 %fusion.4 = f32[20,128,256]{2,1,0:T(8,128)} fusion(bf16[20,128,512]{2,1,0:T(8,128)(2,1)} %gather_fusion.4, pred[20]{0:T(512)(128)(4,1)S(1)} %get-tuple-element.12, s32[20,128]{1,0:T(8,128)S(1)} %bitcast.68, bf16[256,512]{1,0:T(8,128)(2,1)S(1)} %copy-done.8), kind=kOutput, calls=%fused_computation.22 | convolution fusion | flops 841154560 | bytes 5515284 | tf_op jit(solution)/shard_map/beq,bqh->beh/dot_general | solution.py:47
  316.3 3.5 fusion.3
  319.9 0.5 copy-done.17
  320.4 2.4 fusion.5
  322.8 3.2 fusion.31
  326.0 16.6 %scatter_custom_fusion = f32[512,512]{1,0:T(8,128)S(1)} fusion(s32[2560]{0:T(1024)} %param.16, f32[2560,512]{1,0:T(8,128)} %fusion.31, f32[]{:T(128)} %constant.95.clone.1), kind=kCustom, calls=%fused_computation.56 | custom fusion | flops 1310720 | bytes 1049088 | tf_op jit(solution)/shard_map/scatter-add | solution.py:160
  342.5 1.2 fusion.24
  343.7 0.9 convert_element_type.113
  344.6 3.4 fusion.6
  348.0 30.3 %all-reduce.13.cloned.1.call-done = bf16[512,512]{1,0:T(8,128)(2,1)} async-done(((bf16[512,512]{1,0:T(8,128)(2,1)}), bf16[512,512]{1,0:T(8,128)(2,1)}) %all-reduce.13.cloned.1.call-update) | async-done | bytes 524304 | tf_op jit(solution)/shard_map/psum | solution.py:166
  378.4 1.7 fusion.23
  380.1 61.6 %all-reduce.15.cloned.1.call-done = (bf16[1024,256]{1,0:T(8,128)(2,1)}, bf16[256,512]{1,0:T(8,128)(2,1)}, bf16[1024,256]{1,0:T(8,128)(2,1)}, bf16[256,512]{1,0:T(8,128)(2,1)}) async-done(((bf16[1024,256]{1,0:T(8,128)(2,1)}, bf16[256,512]{1,0:T(8,128)(2,1)}, bf16[1024,256]{1,0:T(8,128)(2,1)}, bf16[256,512]{1,0:T(8,128)(2,1)}), (bf16[1024,256]{1,0:T(8,128)(2,1)}, bf16[256,512]{1,0:T(8,128)(2,1)}, ...) | async-done | bytes 1572880 | tf_op jit(solution)/shard_map/psum | solution.py:172
  441.6 2.1 convert_element_type.117
  443.8 2.1 convert_element_type.121
  445.9 0.9 convert_element_type.119
  446.7 0.9 convert_element_type.123
  (68 shorter events, 0.8 us)
Async XLA Ops:
  7.2 152.8 %copy-start = (bf16[1024,256]{1,0:T(8,128)(2,1)S(1)}, bf16[1024,256]{1,0:T(8,128)(2,1)}, u32[]{:S(2)}) copy-start(bf16[1024,256]{1,0:T(8,128)(2,1)} %param.23) | copy-start | bytes 1572868
  11.2 34.0 %all-to-all-start = ((s32[4,1,7]{2,1,0:T(1,128)}), s32[4,1,7]{2,1,0:T(1,128)S(1)}, u32[]{:S(2)}, u32[]{:S(2)}) async-start(s32[4,1,7]{2,1,0:T(1,128)} %bitcast.3), calls=%async_computation | async-start | bytes 4096 | tf_op jit(solution)/shard_map/all_to_all | solution.py:112
  29.4 2.8 copy-start.11
  29.4 2.8 copy-start.16
  32.2 2.9 copy-start.5
  32.2 2.9 copy-start.13
  35.1 2.2 copy-start.8
  36.3 1.1 copy-start.1
  45.2 84.3 %all-to-all-start.1 = ((bf16[4,7,128,512]{3,2,1,0:T(8,128)(2,1)}), bf16[4,7,128,512]{3,2,1,0:T(8,128)(2,1)}, u32[]{:S(2)}, u32[]{:S(2)}) async-start(bf16[4,7,128,512]{3,2,1,0:T(8,128)(2,1)} %select_select_fusion), calls=%async_computation.1 | async-start | bytes 7340032 | tf_op jit(solution)/shard_map/all_to_all | solution.py:111
  49.9 109.1 %all-reduce.7.cloned.1.call-start = ((), (), s32[]{:S(2)}) async-start(), calls=%async_computation.3 | async-start | bytes 524288 | tf_op jit(solution)/shard_map/psum | solution.py:121
  129.5 5.1 %copy-start.19 = (bf16[256]{0:T(256)(128)(2,1)S(1)}, bf16[256]{0:T(256)(128)(2,1)}, u32[]{:S(2)}) copy-start(bf16[256]{0:T(256)(128)(2,1)} %param.24) | copy-start | bytes 1540
  129.5 5.1 %copy-start.7 = (bf16[256,512]{1,0:T(8,128)(2,1)S(1)}, bf16[256,512]{1,0:T(8,128)(2,1)}, u32[]{:S(2)}) copy-start(bf16[256,512]{1,0:T(8,128)(2,1)} %param.15) | copy-start | bytes 786436
  133.7 26.6 %copy-start.18 = (bf16[256,512]{1,0:T(8,128)(2,1)S(1)}, bf16[256,512]{1,0:T(8,128)(2,1)}, u32[]{:S(2)}) copy-start(bf16[256,512]{1,0:T(8,128)(2,1)} %param.25) | copy-start | bytes 786436
  133.7 27.6 %copy-start.14 = (bf16[512]{0:T(512)(128)(2,1)S(1)}, bf16[512]{0:T(512)(128)(2,1)}, u32[]{:S(2)}) copy-start(bf16[512]{0:T(512)(128)(2,1)} %param.26) | copy-start | bytes 3076
  133.7 52.5 %copy-start.3 = (bf16[256,512]{1,0:T(8,128)(2,1)S(1)}, bf16[256,512]{1,0:T(8,128)(2,1)}, u32[]{:S(2)}) copy-start(bf16[256,512]{1,0:T(8,128)(2,1)} %param.27) | copy-start | bytes 786436
  134.5 50.7 %all-reduce.9.cloned.1.call-start = ((), (), s32[]{:S(2)}) async-start(), calls=%async_computation.4 | async-start | bytes 524288 | tf_op jit(solution)/shard_map/psum | solution.py:127
  161.3 54.2 %all-reduce.11.cloned.1.call-start = ((), (), s32[]{:S(2)}) async-start(), calls=%async_computation.5 | async-start | bytes 524288 | tf_op jit(solution)/shard_map/psum | solution.py:148
  191.3 27.8 %copy-start.4 = (f32[256,1024]{1,0:T(8,128)}, f32[256,1024]{1,0:T(8,128)S(1)}, u32[]{:S(2)}) copy-start(f32[256,1024]{1,0:T(8,128)S(1)} %fusion.47) | copy-start | bytes 3145732
  223.4 5.1 %copy-start.15 = (s32[20,1]{0,1:T(1,128)S(1)}, s32[20,1]{0,1:T(1,128)}, u32[]{:S(2)}) copy-start(s32[20,1]{0,1:T(1,128)} %param.18) | copy-start | bytes 244
  223.4 83.9 %all-to-all-start.2 = ((bf16[4,7,128,512]{3,2,1,0:T(8,128)(2,1)}), bf16[4,7,128,512]{3,2,1,0:T(8,128)(2,1)}, u32[]{:S(2)}, u32[]{:S(2)}) async-start(bf16[4,7,128,512]{3,2,1,0:T(8,128)(2,1)} %broadcast_select_fusion), calls=%async_computation.2 | async-start | bytes 7340032 | tf_op jit(solution)/shard_map/all_to_all | solution.py:153
  228.5 149.9 %all-reduce.13.cloned.1.call-start = ((), (), s32[]{:S(2)}) async-start(), calls=%async_computation.6 | async-start | bytes 1048576 | tf_op jit(solution)/shard_map/psum | solution.py:166
  316.3 3.5 copy-start.6
  316.3 4.1 copy-start.17
  320.4 2.4 copy-start.12
  326.0 18.7 %copy-start.2 = (bf16[20,128,256]{2,1,0:T(8,128)(2,1)S(1)}, bf16[20,128,256]{2,1,0:T(8,128)(2,1)}, u32[]{:S(2)}) copy-start(bf16[20,128,256]{2,1,0:T(8,128)(2,1)} %copy-done.1) | copy-start | bytes 3932164
  344.6 97.0 %all-reduce.15.cloned.1.call-start = ((), (), s32[]{:S(2)}) async-start(), calls=%async_computation.7 | async-start | bytes 3145728 | tf_op jit(solution)/shard_map/psum | solution.py:172
  441.6 4.2 copy-start.10
  441.6 5.1 %copy-start.9 = (bf16[256,512]{1,0:T(8,128)(2,1)S(1)}, bf16[256,512]{1,0:T(8,128)(2,1)}, u32[]{:S(2)}) copy-start(bf16[256,512]{1,0:T(8,128)(2,1)} %get-tuple-element.11) | copy-start | bytes 786436
Sparse Core Ops, SparseCore 0:
  134.6 24.3 all-reduce.6
  162.0 23.1 all-reduce.8
  192.3 23.1 all-reduce.10
  344.7 33.5 all-reduce.12
  381.6 60.0 all-reduce.14
where the time goes:
time: 460 us; the launch traced here: 454 us
  waiting for transfers between devices  318 us (69%)
  other arithmetic  51.8 us (11%)
  matrix products  26.7 us (6%)
  local copies, waits for them, and re-layouts  25.5 us (6%)
  starting transfers between devices  14.5 us (3%)
  between operations  14.1 us (3%)
    all_to_all x1, waiting for transfers between devices, on_device(): lax.all_to_all(outgoing, 'region', split_axis=0, concat_axis=0, tiled=True)  78.2 us
    all_to_all x1, waiting for transfers between devices, on_device(): lax.all_to_all(replies, 'region', split_axis=0, concat_axis=0, tiled=True)  76.6 us
    psum x1, waiting for transfers between devices, on_device(): lax.psum(grad_edge_in.astype(jnp.bfloat16), ('region', 'sub'))  61.6 us
    psum x1, waiting for transfers between devices, on_device(): lax.psum(sender_part.astype(jnp.bfloat16), ('hid', 'sub'))  30.3 us
    psum x1, waiting for transfers between devices, on_device(): lax.psum(partial_agg.reshape(node_rows, latent).astype(jnp.bfloat16), 'hid')  24.4 us
    psum x1, waiting for transfers between devices, on_device(): lax.psum(jnp.dot(node_hidden, w_node_out, preferred_element_type=jnp.floa...  23.7 us
    psum x1, waiting for transfers between devices, on_device(): lax.psum(grad_node_cat[:, latent:].astype(jnp.bfloat16), 'hid')  23.3 us
    scatter-add x1, other arithmetic, on_device(): jax.ops.segment_sum(grad_send, senders, num_segments=region_nodes.shape[0])  16.6 us
  transfers between devices with their start and end apart: 8, of which 7 were waited for; matrix products, arithmetic and copies ran while one was open for 7% of the time, Pallas kernels for 0%

commit v1 on v0

v1 whole, which is shorter than its diff:
```python
import functools
import jax
import jax.numpy as jnp
from jax import lax
from jax.experimental import pallas as pl
from jax.experimental.pallas import tpu as pltpu
from jax.sharding import PartitionSpec as P

F32 = jnp.float32
BF16 = jnp.bfloat16
MESH = pl.DeviceIdType.MESH
VMEM_BYTES = 48 * 1024 * 1024


def dot(a, b):
    return jnp.dot(a, b, preferred_element_type=F32)


def dot_t(a, b):
    return lax.dot_general(a, b, (((1,), (1,)), ((), ())), preferred_element_type=F32)


def t_dot(a, b):
    return lax.dot_general(a, b, (((0,), (0,)), ((), ())), preferred_element_type=F32)


def logistic(v):
    return 1.0 / (1.0 + jnp.exp(-v))


def edge_forward_kernel(
    block_rows, per_step, codes, lat, send, slot, own_part, other_part, w_lat, bias, agg, slope, total
):
    step = pl.program_id(0)
    edges = lat.shape[0]
    nodes = own_part.shape[0]

    @pl.when(step == 0)
    def _():
        total[...] = jnp.zeros_like(total)

    places = lax.broadcasted_iota(jnp.int32, (nodes, edges), 0)
    ids = send[0]
    pre = dot(lat[...], w_lat[...]) + bias[...].astype(F32)
    pre += t_dot((places == ids).astype(BF16), own_part[...])
    pre += t_dot((places + nodes == ids).astype(BF16), other_part[...])
    gate = logistic(pre)
    hidden = (pre * gate).astype(BF16)
    slope[...] = (gate * (1.0 + pre * (1.0 - gate))).astype(BF16)
    rows = lax.broadcasted_iota(jnp.int32, (block_rows, block_rows), 0)
    for j in range(per_step):
        at = slice(j * block_rows, (j + 1) * block_rows)
        pick = (rows == slot[0, :, at]).astype(BF16)
        to = pl.ds(pl.multiple_of(codes[step * per_step + j] * block_rows, block_rows), block_rows)
        total[to, :] += dot(pick, hidden[at])

    @pl.when(step == pl.num_programs(0) - 1)
    def _():
        agg[...] = total[...].astype(BF16)


def edge_backward_kernel(
    block_rows, per_step, codes, lat, send, slot, grads, slope, grad_lat, grad_own, grad_other
):
    step = pl.program_id(0)
    edges = lat.shape[0]
    nodes = grad_own.shape[0]

    @pl.when(step == 0)
    def _():
        grad_lat[...] = jnp.zeros_like(grad_lat)
        grad_own[...] = jnp.zeros_like(grad_own)
        grad_other[...] = jnp.zeros_like(grad_other)

    rows = lax.broadcasted_iota(jnp.int32, (block_rows, block_rows), 0)
    parts = []
    for j in range(per_step):
        at = slice(j * block_rows, (j + 1) * block_rows)
        pick = (rows == slot[0, :, at]).astype(BF16)
        to = pl.ds(pl.multiple_of(codes[step * per_step + j] * block_rows, block_rows), block_rows)
        parts.append((t_dot(pick, grads[to, :]) * slope[at].astype(F32)).astype(BF16))
    grad_pre = jnp.concatenate(parts, axis=0)
    grad_lat[...] += t_dot(lat[...], grad_pre)
    places = lax.broadcasted_iota(jnp.int32, (nodes, edges), 0)
    ids = send[0]
    grad_own[...] += dot((places == ids).astype(BF16), grad_pre)
    grad_other[...] += dot((places + nodes == ids).astype(BF16), grad_pre)


def node_kernel(
    agg, nodes, cot, weo, wni, bn, wno, gain,
    gathered_o, hidden_o, gu_o, gnp_o, gg_o, new_o, cat_o,
):
    latent = nodes.shape[1]
    gathered = dot(agg[...], weo[...]).astype(BF16)
    gathered_o[...] = gathered
    lat = nodes[...]
    pre = dot(lat, wni[:latent]) + dot(gathered, wni[latent:]) + bn[...].astype(F32)
    gate = logistic(pre)
    hidden = (pre * gate).astype(BF16)
    slope = gate * (1.0 + pre * (1.0 - gate))
    hidden_o[...] = hidden
    update = dot(hidden, wno[...])
    scale = gain[...].astype(F32)
    centred = update - jnp.mean(update, axis=-1, keepdims=True)
    inv = lax.rsqrt(jnp.mean(centred * centred, axis=-1, keepdims=True) + 1e-05)
    unit = centred * inv
    new_o[...] = (lat.astype(F32) + unit * scale).astype(BF16)
    cot_gain = cot[...].astype(F32) * scale
    grad = cot_gain - jnp.mean(cot_gain, axis=-1, keepdims=True)
    grad = (grad - unit * jnp.mean(cot_gain * unit, axis=-1, keepdims=True)) * inv
    grad = grad.astype(BF16)
    gu_o[...] = grad
    gnp = (dot_t(grad, wno[...]) * slope).astype(BF16)
    gnp_o[...] = gnp
    cat = dot_t(gnp, wni[...])
    cat_o[...] = cat[:, :latent].astype(BF16)
    gg_o[...] = cat[:, latent:].astype(BF16)


def reduce_kernel(
    regions, value, out, from_sub, shared, half_sum, from_region, piece, gathered,
    sub_send, sub_recv, rs_send, rs_recv, ag_send, ag_recv, share_send, share_recv,
):
    me = lax.axis_index("region")
    sub = lax.axis_index("sub")
    other = 1 - sub
    half = value.shape[0] // 2
    chunk = half // regions
    barrier = pltpu.get_barrier_semaphore()
    pl.semaphore_signal(barrier, inc=1, device_id={"sub": other}, device_id_type=MESH)
    for j in range(1, regions):
        pl.semaphore_signal(
            barrier, inc=1, device_id={"region": lax.rem(me + j, regions)}, device_id_type=MESH
        )
    pl.semaphore_wait(barrier, regions)

    def rows(index, size):
        return pl.ds(pl.multiple_of(index * size, 16), size)

    first = pltpu.make_async_remote_copy(
        value.at[rows(other, half), :], from_sub, sub_send, sub_recv,
        device_id={"sub": other}, device_id_type=MESH,
    )
    first.start()
    first.wait()
    half_sum[...] = (value[rows(sub, half), :].astype(F32) + from_sub[...].astype(F32)).astype(BF16)
    sends = []
    for j in range(1, regions):
        to = lax.rem(me + j, regions)
        copy = pltpu.make_async_remote_copy(
            half_sum.at[rows(to, chunk), :], from_region.at[j], rs_send.at[j], rs_recv.at[j],
            device_id={"region": to}, device_id_type=MESH,
        )
        copy.start()
        sends.append(copy)
    total = half_sum[rows(me, chunk), :].astype(F32)
    for j in range(1, regions):
        sends[j - 1].wait_recv()
        total = total + from_region[j].astype(F32)
    piece[...] = total.astype(BF16)
    gathers = []
    for j in range(1, regions):
        to = lax.rem(me + j, regions)
        copy = pltpu.make_async_remote_copy(
            piece, gathered.at[j], ag_send.at[j], ag_recv.at[j],
            device_id={"region": to}, device_id_type=MESH,
        )
        copy.start()
        gathers.append(copy)
    shares = []
    base = half
    for j in range(regions):
        if j:
            gathers[j - 1].wait_recv()
            source = gathered.at[j]
        else:
            source = piece
        copy = pltpu.make_async_remote_copy(
            source, shared.at[pl.ds(j * chunk, chunk), :], share_send.at[j], share_recv.at[j],
            device_id={"sub": other}, device_id_type=MESH,
        )
        copy.start()
        shares.append(copy)
        origin = lax.rem(me - j + regions, regions)
        out[rows(sub * regions + origin, chunk), :] = source[...].astype(F32)
    for j in range(regions):
        shares[j].wait_recv()
        origin = lax.rem(me - j + regions, regions)
        out[rows(other * regions + origin, chunk), :] = shared[j * chunk:(j + 1) * chunk, :].astype(F32)
    first_done = sends + gathers + shares
    for copy in first_done:
        copy.wait_send()


def reduce_over(value, regions, collective_id):
    half = value.shape[0] // 2
    chunk = half // regions
    width = value.shape[1]
    dma = pltpu.SemaphoreType.DMA
    return pl.pallas_call(
        functools.partial(reduce_kernel, regions),
        out_shape=jax.ShapeDtypeStruct(value.shape, F32),
        in_specs=[pl.BlockSpec(memory_space=pltpu.VMEM)],
        out_specs=pl.BlockSpec(memory_space=pltpu.VMEM),
        scratch_shapes=[
            pltpu.VMEM((half, width), BF16),
            pltpu.VMEM((half, width), BF16),
            pltpu.VMEM((half, width), BF16),
            pltpu.VMEM((regions, chunk, width), BF16),
            pltpu.VMEM((chunk, width), BF16),
            pltpu.VMEM((regions, chunk, width), BF16),
            dma, dma, dma((regions,)), dma((regions,)), dma((regions,)), dma((regions,)),
            dma((regions,)), dma((regions,)),
        ],
        compiler_params=pltpu.CompilerParams(
            collective_id=collective_id, has_side_effects=True, vmem_limit_bytes=VMEM_BYTES
        ),
    )(value)


def on_device(
    edge_lat,
    node_lat,
    senders,
    recv_slots,
    owners,
    targets,
    w_edge_in,
    b_edge,
    w_edge_out,
    w_node_in,
    b_node,
    w_node_out,
    norm_gain,
    cotangent,
):
    regions = lax.axis_size("region")
    me = lax.axis_index("region")
    hid = lax.axis_index("hid")
    sub = lax.axis_index("sub")
    blocks = owners.shape[0]
    edges = edge_lat.shape[0]
    block_rows = edges // blocks
    node_rows, latent = node_lat.shape
    width = w_edge_in.shape[1]
    recv_blocks = node_rows // block_rows
    hids = lax.axis_size("hid")
    share = node_rows // hids
    per_step = 4 if blocks % 4 == 0 else 1
    steps = blocks // per_step
    span = per_step * block_rows

    def swap(value, axis):
        return lax.ppermute(value, axis, [(0, 1), (1, 0)])

    def hid_shift(value, by):
        return lax.ppermute(value, "hid", [(i, (i + by) % hids) for i in range(hids)])

    def hid_all(value, axis=0):
        return jnp.concatenate([value] + [hid_shift(value, j) for j in range(1, hids)], axis=axis)

    def ordered(parts):
        descending = parts[::-1]
        rows = parts[0].shape[0]
        doubled = jnp.concatenate(descending + descending[:-1], axis=0)
        return lax.dynamic_slice_in_dim(doubled, (hids - 1 - hid) * rows, hids * rows, 0)

    def hid_ordered(value):
        return ordered([value] + [hid_shift(value, j) for j in range(1, hids)])

    def hid_sum(value):
        total = value.astype(F32)
        for j in range(1, hids):
            total = total + hid_shift(value, j).astype(F32)
        return total

    def shift(value, by):
        return lax.ppermute(value, "region", [(i, (i + by) % regions) for i in range(regions)])

    weo = hid_all(w_edge_out)
    wni = hid_all(w_node_in, 1)
    wno = hid_all(w_node_out)
    bn = hid_all(b_node)

    own_part = jnp.dot(node_lat, w_edge_in[latent:], preferred_element_type=F32).astype(BF16)
    other_part = swap(own_part, "sub")

    owner = owners[:, 0]
    ahead = lax.rem(owner - me + regions, regions) * recv_blocks + targets
    behind = lax.rem(me - owner + regions, regions) * recv_blocks + targets
    send_rows = jnp.bitwise_xor(senders // node_rows, sub) * node_rows + senders % node_rows
    send_rows = send_rows.reshape(steps, 1, span)
    slots = recv_slots.reshape(steps, 1, span)
    whole = lambda *shape: pl.BlockSpec(shape, lambda i, c: (0,) * len(shape))
    tile = lambda cols: pl.BlockSpec((span, cols), lambda i, c: (i, 0))
    ids = pl.BlockSpec((1, 1, span), lambda i, c: (i, 0, 0))
    params = pltpu.CompilerParams(vmem_limit_bytes=VMEM_BYTES)
    agg_rows = regions * node_rows

    agg, slope = pl.pallas_call(
        functools.partial(edge_forward_kernel, block_rows, per_step),
        out_shape=(
            jax.ShapeDtypeStruct((agg_rows, width), BF16),
            jax.ShapeDtypeStruct((edges, width), BF16),
        ),
        grid_spec=pltpu.PrefetchScalarGridSpec(
            num_scalar_prefetch=1,
            grid=(steps,),
            in_specs=[
                tile(latent), ids, ids, whole(node_rows, width), whole(node_rows, width),
                whole(latent, width), whole(1, width),
            ],
            out_specs=[whole(agg_rows, width), tile(width)],
            scratch_shapes=[pltpu.VMEM((agg_rows, width), F32)],
        ),
        compiler_params=params,
    )(ahead, edge_lat, send_rows, slots, own_part, other_part, w_edge_in[:latent], b_edge[None])

    agg = agg.reshape(regions, node_rows, width)
    gathered_k = agg[0].astype(F32)
    for arrived in [shift(agg[j], j) for j in range(1, regions)]:
        gathered_k = gathered_k + arrived.astype(F32)
    gathered_k = gathered_k.astype(BF16)

    def rows_of(value, by):
        at = lax.rem(hid + by, hids) * share
        return lax.dynamic_slice_in_dim(value, at, share, 0)

    agg_mine = jnp.concatenate(
        [rows_of(gathered_k, 0)]
        + [hid_shift(rows_of(gathered_k, j), j) for j in range(1, hids)],
        axis=1,
    )
    row = lambda cols: jax.ShapeDtypeStruct((share, cols), BF16)
    all_units = hids * width
    gathered, hidden, gu, gnp, gg, new_rows, cat = pl.pallas_call(
        node_kernel,
        out_shape=(
            row(latent), row(all_units), row(latent), row(all_units), row(latent), row(latent),
            row(latent),
        ),
        compiler_params=params,
    )(
        agg_mine, rows_of(node_lat, 0), rows_of(cotangent, 0), weo, wni, bn[None], wno,
        norm_gain[None],
    )
    gg_all = hid_ordered(gg)
    gs = dot_t(gg_all, w_edge_out).astype(BF16)
    gs_all = jnp.concatenate([gs] + [shift(gs, j) for j in range(1, regions)], axis=0)

    new_nodes = hid_ordered(new_rows)
    packs = []
    for j in range(hids):
        at = (hids - j) % hids * width
        pack = jnp.concatenate(
            [gathered, gu, hidden[:, at:at + width], gnp[:, at:at + width]], axis=1
        )
        packs.append(hid_shift(pack, j) if j else pack)
    packed = ordered(packs)
    gathered_all = packed[:, :latent]
    gu_all = packed[:, latent:2 * latent]
    hid_rows = packed[:, 2 * latent:2 * latent + width]
    gnp_all = packed[:, 2 * latent + width:]
    grad_node_in = t_dot(jnp.concatenate([node_lat, gathered_all], axis=1), gnp_all)
    grad_node_out = t_dot(hid_rows, gu_all)
    grad_edge_out = t_dot(gathered_k, gg_all)

    grad_lat, grad_own, grad_other = pl.pallas_call(
        functools.partial(edge_backward_kernel, block_rows, per_step),
        out_shape=(
            jax.ShapeDtypeStruct((latent, width), F32),
            jax.ShapeDtypeStruct((node_rows, width), F32),
            jax.ShapeDtypeStruct((node_rows, width), F32),
        ),
        grid_spec=pltpu.PrefetchScalarGridSpec(
            num_scalar_prefetch=1,
            grid=(steps,),
            in_specs=[tile(latent), ids, ids, whole(agg_rows, width), tile(width)],
            out_specs=[whole(latent, width), whole(node_rows, width), whole(node_rows, width)],
        ),
        compiler_params=params,
    )(behind, edge_lat, send_rows, slots, gs_all, slope)

    grad_send = (grad_own + swap(grad_other.astype(BF16), "sub").astype(F32)).astype(BF16)
    node_part = dot_t(grad_send, w_edge_in[latent:])
    cat_rows = lax.dynamic_update_slice_in_dim(
        jnp.zeros((node_rows, latent), BF16), cat, hid * share, 0
    )
    node_part = (node_part + cat_rows.astype(F32)).astype(BF16)
    grad_nodes = (cotangent.astype(F32) + hid_sum(node_part)).astype(BF16)

    def tall(value):
        value = value.astype(BF16)
        return [value[:, at:at + width] for at in range(0, latent, width)]

    stacked = jnp.concatenate(
        [grad_node_in.astype(BF16)]
        + tall(grad_node_out)
        + tall(grad_edge_out)
        + [grad_lat.astype(BF16), t_dot(node_lat, grad_send).astype(BF16)],
        axis=0,
    )
    reduced = reduce_over(stacked, regions, 1)

    def flat(at):
        return jnp.concatenate(
            [reduced[at + step:at + step + width] for step in range(0, latent, width)], axis=1
        )

    return (
        new_nodes,
        grad_nodes,
        reduced[4 * latent:],
        flat(3 * latent),
        reduced[:2 * latent],
        flat(2 * latent),
    )


def solution(mesh):
    placed = (
        P(("group", "region", "sub"), None),
        P(("group", "region", "sub"), None),
        P(("group", "region", "sub")),
        P(("group", "region", "sub")),
        P(("group", "region", "sub"), None),
        P(("group", "region", "sub")),
        P(None, "hid"),
        P("hid"),
        P("hid", None),
        P(None, "hid"),
        P("hid"),
        P("hid", None),
        P(),
        P(("group", "region", "sub"), None),
    )
    return jax.shard_map(
        on_device,
        mesh=mesh,
        in_specs=placed,
        out_specs=(
            P(("group", "region", "sub"), None),
            P(("group", "region", "sub"), None),
            P("group", "hid"),
            P(("group", "hid"), None),
            P("group", "hid"),
            P(("group", "hid"), None),
        ),
        check_vma=False,
    )
```

time: 460 us -> 120 us (0.26); the launches traced: 454 us -> 120 us
  waiting for transfers between devices: 318 us -> 19.3 us
  Pallas kernels: 0 us -> 54.7 us
  other arithmetic: 51.8 us -> 10.6 us
  matrix products: 26.7 us -> 2.89 us
  local copies, waits for them, and re-layouts: 25.5 us -> 7.5 us
  between operations: 14.1 us -> 1.06 us
  starting transfers between devices: 14.5 us -> 23.9 us
    psum x5 -> x0, waiting for transfers between devices: 163 us -> none  [the longest x1 61.6 us: on_device(): lax.psum(grad_edge_in.astype(jnp.bfloat16), ('region', 'sub'))]
    all_to_all x3 -> x0, waiting for transfers between devices: 155 us -> none  [the longest x1 78.2 us: on_device(): lax.all_to_all(outgoing, 'region', split_axis=0, concat_axis=0, tiled=True)]
    pallas_call x0 -> x4, Pallas kernels: none -> 54.7 us  [the longest x1 44.6 us: reduce_over(): pl.pallas_call(functools.partial(reduce_kernel, regions), out_shape=jax.S...]
    ppermute x0 -> x17, starting transfers between devices: none -> 23.9 us  [the longest x9 9.44 us: hid_shift(): lax.ppermute(value, 'hid', [(i, (i + by) % hids) for i in range(hids)])]
    dot_general x14 -> x7, matrix products: 26.7 us -> 2.89 us  [the longest x1 1.26 us: on_device(): jnp.dot(node_lat, w_edge_in[latent:], preferred_element_type=F32)]
    gather x6 -> x0, local copies, waits for them, and re-layouts: 20.3 us -> none  [the longest x1 8.19 us: edge_forward(): jnp.take(region_nodes, send_ids, axis=0)]
    ppermute x0 -> x17, waiting for transfers between devices: none -> 19.3 us  [the longest x6 12.5 us: shift(): lax.ppermute(value, 'region', [(i, (i + by) % regions) for i in range(reg...]
    scatter-add x1 -> x0, other arithmetic: 16.6 us -> none  [on_device(): jax.ops.segment_sum(grad_send, senders, num_segments=region_nodes.shape[0])]
  transfers between devices with their start and end apart: 8 -> 17, of which waited for: 7 -> 7; matrix products, arithmetic and copies ran while one was open for 7% -> 15% of each run, Pallas kernels for 0% -> 44%
where the time goes in v1:
time: 120 us
  Pallas kernels  54.7 us (46%)
  starting transfers between devices  23.9 us (20%)
  waiting for transfers between devices  19.3 us (16%)
  other arithmetic  10.6 us (9%)
  local copies, waits for them, and re-layouts  7.5 us (6%)
  matrix products  2.89 us (2%)
    pallas_call x1, Pallas kernels, reduce_over(): pl.pallas_call(functools.partial(reduce_kernel, regions), out_shape=jax.S...  44.6 us
    ppermute x6, waiting for transfers between devices, shift(): lax.ppermute(value, 'region', [(i, (i + by) % regions) for i in range(reg...  12.5 us
    ppermute x9, starting transfers between devices, hid_shift(): lax.ppermute(value, 'hid', [(i, (i + by) % hids) for i in range(hids)])  9.44 us
    ppermute x2, starting transfers between devices, swap(): return lax.ppermute(value, axis, [(0, 1), (1, 0)])  8.45 us
    ppermute x9, waiting for transfers between devices, hid_shift(): lax.ppermute(value, 'hid', [(i, (i + by) % hids) for i in range(hids)])  6.73 us
    ppermute x6, starting transfers between devices, shift(): lax.ppermute(value, 'region', [(i, (i + by) % regions) for i in range(reg...  6 us
    concatenate x3, other arithmetic, ordered(): doubled = jnp.concatenate(descending + descending[:-1], axis=0)  5.45 us
    pallas_call x1, Pallas kernels, on_device(): pl.pallas_call(functools.partial(edge_forward_kernel, block_rows, per_ste...  4.47 us
  transfers between devices with their start and end apart: 17, of which 7 were waited for; matrix products, arithmetic and copies ran while one was open for 15% of the time, Pallas kernels for 44%

profile of v1, /device:TPU:25, one launch (start us, length us, event | category | flops | bytes accessed | tf_op | source)
XLA Modules:
  0.0 120.0 jit_solution(15858459400619883743)
XLA Ops:
  0.6 1.3 %collective-permute-start.7 = (bf16[256]{0:T(256)(128)(2,1)}, bf16[256]{0:T(256)(128)(2,1)S(1)}, u32[]{:S(2)}, u32[]{:S(2)}) collective-permute-start(bf16[256]{0:T(256)(128)(2,1)} %param.24), channel_id=1, source_target_pairs={{0,2},{2,0},{1,3},{3,1},{4,6},{6,4},{5,7},{7,5},{8,10},{10,8},{9,1... | collective-permute-start | bytes 1544 | tf_op jit(solution)/shard_map/ppermute | solution.py:258
  1.9 1.3 %convolution_convert_fusion.5.own_part = bf16[256,256]{1,0:T(8,128)(2,1)S(1)} fusion(bf16[256,512]{1,0:T(8,128)(2,1)} %param.15, bf16[1024,256]{1,0:T(8,128)(2,1)} %param.20), kind=kOutput, calls=%fused_computation.16 | convolution fusion | flops 67174400 | bytes 655360 | tf_op jit(solution)/shard_map/dot_general | solution.py:286
  3.2 1.0 collective-permute-start
  4.2 0.3 collective-permute-start.8
  4.5 0.7 fusion.23
  5.2 0.7 fusion.33
  5.9 1.0 slice.78.w_lat
  6.8 0.7 broadcast_in_dim.12.bias
  7.5 0.7 reshape.36.slot
  8.3 0.9 constant_dynamic-slice_fusion.1.nodes
  9.2 0.0 copy-start
  9.2 1.7 %copy-done = bf16[2560,512]{1,0:T(8,128)(2,1)S(1)} copy-done((bf16[2560,512]{1,0:T(8,128)(2,1)S(1)}, bf16[2560,512]{1,0:T(8,128)(2,1)}, u32[]{:S(2)}) %copy-start) | copy-done | bytes 2621464
  10.9 4.5 %shard_map.181 = (bf16[1024,256]{1,0:T(8,128)(2,1)S(1)}, bf16[2560,256]{1,0:T(8,128)(2,1)S(1)}) custom-call(s32[20]{0:T(128)S(1)} %get-tuple-element.46.codes, bf16[2560,512]{1,0:T(8,128)(2,1)S(1)} %copy-done, s32[5,1,512]{2,1,0:T(1,128)S(1)} %reshape.35.send, s32[5,1,512]{2,1,0:T(1,128)S(1)} %reshape.36.slot, ...), custom_call_target="tpu_custom_call" | custom-call | tf_op jit(solution)/shard_map/pallas_call | solution.py:301
  15.4 0.0 copy-start.7
  15.4 0.8 fusion.37
  16.2 0.0 collective-permute-start.1
  16.2 1.5 %collective-permute-start.3 = (bf16[256,256]{1,0:T(8,128)(2,1)}, bf16[256,256]{1,0:T(8,128)(2,1)S(1)}, u32[]{:S(2)}, u32[]{:S(2)}) collective-permute-start(bf16[256,256]{1,0:T(8,128)(2,1)} %get-tuple-element.37), channel_id=1, source_target_pairs={{0,12},{4,0},{8,4},{12,8},{1,13},{5,1},{9,5},{13,9},{2,14},{6,2},{... | collective-permute-start | bytes 393224 | tf_op jit(solution)/shard_map/ppermute | solution.py:279
  17.7 0.1 collective-permute-start.2
  17.8 0.0 collective-permute-done.7
  17.8 1.3 %collective-permute-start.5 = (bf16[256,512]{1,0:T(8,128)(2,1)S(1)}, bf16[256,512]{1,0:T(8,128)(2,1)S(1)}, u32[]{:S(2)}, u32[]{:S(2)}) collective-permute-start(bf16[256,512]{1,0:T(8,128)(2,1)S(1)} %copy-done.4), channel_id=1, source_target_pairs={{0,2},{2,0},{1,3},{3,1},{4,6},{6,4},{5,7},{7,5},{8,10},{10,8},{9,1... | collective-permute-start | bytes 786440 | tf_op jit(solution)/shard_map/ppermute | solution.py:258
  19.1 0.0 copy-start.6
  19.1 2.2 %collective-permute-done.1 = bf16[256,256]{1,0:T(8,128)(2,1)S(1)} collective-permute-done((bf16[256,256]{1,0:T(8,128)(2,1)}, bf16[256,256]{1,0:T(8,128)(2,1)S(1)}, u32[]{:S(2)}, u32[]{:S(2)}) %collective-permute-start.1) | collective-permute-done | bytes 131104 | tf_op jit(solution)/shard_map/ppermute | solution.py:279
  21.3 1.2 %collective-permute-start.6 = (bf16[1024,256]{1,0:T(8,128)(2,1)}, bf16[1024,256]{1,0:T(8,128)(2,1)S(1)}, u32[]{:S(2)}, u32[]{:S(2)}) collective-permute-start(bf16[1024,256]{1,0:T(8,128)(2,1)} %param.23), channel_id=1, source_target_pairs={{0,2},{2,0},{1,3},{3,1},{4,6},{6,4},{5,7},{7,5},{8,10},{10,8},{9,1... | collective-permute-start | bytes 1572872 | tf_op jit(solution)/shard_map/ppermute | solution.py:258
  22.6 1.2 %collective-permute-done.3 = bf16[256,256]{1,0:T(8,128)(2,1)S(1)} collective-permute-done((bf16[256,256]{1,0:T(8,128)(2,1)}, bf16[256,256]{1,0:T(8,128)(2,1)S(1)}, u32[]{:S(2)}, u32[]{:S(2)}) %collective-permute-start.3) | collective-permute-done | bytes 131104 | tf_op jit(solution)/shard_map/ppermute | solution.py:279
  23.8 6.0 %collective-permute-done.2 = bf16[256,256]{1,0:T(8,128)(2,1)} collective-permute-done((bf16[256,256]{1,0:T(8,128)(2,1)}, bf16[256,256]{1,0:T(8,128)(2,1)}, u32[]{:S(2)}, u32[]{:S(2)}) %collective-permute-start.2) | collective-permute-done | bytes 131104 | tf_op jit(solution)/shard_map/ppermute | solution.py:279
  29.8 1.0 add_convert_fusion.2
  30.8 1.3 %collective-permute-start.4 = (bf16[128,256]{1,0:T(8,128)(2,1)S(1)}, bf16[128,256]{1,0:T(8,128)(2,1)S(1)}, u32[]{:S(2)}, u32[]{:S(2)}) collective-permute-start(bf16[128,256]{1,0:T(8,128)(2,1)S(1)} %get-tuple-element.44), channel_id=1, source_target_pairs={{0,2},{2,0},{1,3},{3,1},{4,6},{6,4},{5,7},{7,5},{8,10},{10,8},{9,1... | collective-permute-start | bytes 196616 | tf_op jit(solution)/shard_map/ppermute | solution.py:258
  32.1 0.0 collective-permute-done.8
  32.1 0.0 collective-permute-done.5
  32.2 4.4 %collective-permute-done.4 = bf16[128,256]{1,0:T(8,128)(2,1)S(1)} collective-permute-done((bf16[128,256]{1,0:T(8,128)(2,1)S(1)}, bf16[128,256]{1,0:T(8,128)(2,1)S(1)}, u32[]{:S(2)}, u32[]{:S(2)}) %collective-permute-start.4) | collective-permute-done | bytes 65568 | tf_op jit(solution)/shard_map/ppermute | solution.py:258
  36.6 0.1 pad_maximum_fusion.wni
  36.6 1.6 %shard_map.182 = (bf16[128,512]{1,0:T(8,128)(2,1)S(1)}, bf16[128,512]{1,0:T(8,128)(2,1)S(1)}, bf16[128,512]{1,0:T(8,128)(2,1)S(1)}, bf16[128,512]{1,0:T(8,128)(2...) custom-call(bf16[128,512]{1,0:T(8,128)(2,1)S(1)} %pad_maximum_fusion.7.agg, ...), custom_call_target="tpu_custom_call" | custom-call | tf_op jit(solution)/shard_map/pallas_call | solution.py:337
  38.3 1.3 %collective-permute-start.9 = (bf16[128,512]{1,0:T(8,128)(2,1)S(1)}, bf16[128,512]{1,0:T(8,128)(2,1)S(1)}, u32[]{:S(2)}, u32[]{:S(2)}) collective-permute-start(bf16[128,512]{1,0:T(8,128)(2,1)S(1)} %get-tuple-element.19), channel_id=1, source_target_pairs={{0,2},{2,0},{1,3},{3,1},{4,6},{6,4},{5,7},{7,5},{8,10},{10,8},{9,1... | collective-permute-start | bytes 393224 | tf_op jit(solution)/shard_map/ppermute | solution.py:258
  39.6 0.2 collective-permute-start.10
  39.9 1.3 %collective-permute-start.16 = (bf16[128,1536]{1,0:T(8,128)(2,1)S(1)}, bf16[128,1536]{1,0:T(8,128)(2,1)S(1)}, u32[]{:S(2)}, u32[]{:S(2)}) collective-permute-start(bf16[128,1536]{1,0:T(8,128)(2,1)S(1)} %pad_maximum_fusion.6), channel_id=1, source_target_pairs={{0,2},{2,0},{1,3},{3,1},{4,6},{6,4},{5,7},{7,5},{8,10},{10,8},{9,1... | collective-permute-start | bytes 1179656 | tf_op jit(solution)/shard_map/ppermute | solution.py:258
  41.2 2.4 %collective-permute-done.10 = bf16[128,512]{1,0:T(8,128)(2,1)S(1)} collective-permute-done((bf16[128,512]{1,0:T(8,128)(2,1)S(1)}, bf16[128,512]{1,0:T(8,128)(2,1)S(1)}, u32[]{:S(2)}, u32[]{:S(2)}) %collective-permute-start.10) | collective-permute-done | bytes 131104 | tf_op jit(solution)/shard_map/ppermute | solution.py:258
  43.6 0.4 fusion.13
  44.0 0.0 copy-start.1
  44.0 0.3 convolution_convert_fusion.4
  44.3 0.5 collective-permute-start.13
  44.8 3.1 %collective-permute-start.12 = (bf16[256,256]{1,0:T(8,128)(2,1)S(1)}, bf16[256,256]{1,0:T(8,128)(2,1)S(1)}, u32[]{:S(2)}, u32[]{:S(2)}) collective-permute-start(bf16[256,256]{1,0:T(8,128)(2,1)S(1)} %convolution_convert_fusion.4), channel_id=1, source_target_pairs={{0,8},{4,12},{8,0},{12,4},{1,9},{5,13},{9,1},{13,5},{2,10},{6,14},... | collective-permute-start | bytes 393224 | tf_op jit(solution)/shard_map/ppermute | solution.py:279
  47.9 0.9 collective-permute-start.11
  48.8 0.2 convolution_convert_fusion.2
  49.0 1.2 fusion.15
  50.2 0.0 collective-permute-done.13
  50.2 2.7 %collective-permute-done.12 = bf16[256,256]{1,0:T(8,128)(2,1)S(1)} collective-permute-done((bf16[256,256]{1,0:T(8,128)(2,1)S(1)}, bf16[256,256]{1,0:T(8,128)(2,1)S(1)}, u32[]{:S(2)}, u32[]{:S(2)}) %collective-permute-start.12) | collective-permute-done | bytes 131104 | tf_op jit(solution)/shard_map/ppermute | solution.py:279
  52.9 0.4 collective-permute-done.11
  53.3 4.0 %shard_map.183 = (f32[512,256]{1,0:T(8,128)S(1)}, f32[256,256]{1,0:T(8,128)S(1)}, f32[256,256]{1,0:T(8,128)S(1)}) custom-call(s32[20]{0:T(128)S(1)} %get-tuple-element.45.codes, bf16[2560,512]{1,0:T(8,128)(2,1)S(1)} %copy-done.1, s32[5,1,512]{2,1,0:T(1,128)S(1)} %reshape.35.send, s32[5,1,512]{2,1,0:T(1,128)S(1)} %reshape.36.slot, ...), custom_call_target="tpu_custom_call" | custom-call | tf_op jit(solution)/shard_map/pallas_call | solution.py:369
  57.3 0.0 copy-start.3
  57.4 7.4 %collective-permute-start.14 = (bf16[256,256]{1,0:T(8,128)(2,1)S(1)}, bf16[256,256]{1,0:T(8,128)(2,1)S(1)}, u32[]{:S(2)}, u32[]{:S(2)}) collective-permute-start(bf16[256,256]{1,0:T(8,128)(2,1)S(1)} %convert_element_type.74), channel_id=1, source_target_pairs={{0,1},{1,0},{2,3},{3,2},{4,5},{5,4},{6,7},{7,6},{8,9},{9,8},{10,11... | collective-permute-start | bytes 393224 | tf_op jit(solution)/shard_map/ppermute | solution.py:255
  64.8 0.0 collective-permute-done.16
  64.8 3.8 %fusion.5 = bf16[256,1536]{1,0:T(8,128)(2,1)S(1)} fusion(s32[]{:T(128)S(6)} %select_n.32, bf16[128,1536]{1,0:T(8,128)(2,1)S(1)} %collective-permute-done.16, bf16[128,512]{1,0:T(8,128)(2,1)S(1)} %get-tuple-element.25, bf16[128,512]{1,0:T(8,128)(2,1)S(1)} %get-tuple-element.26, bf16[128,256]{1,0:T(8,128)(2,1)S(1)} %get-tuple-element.48, ...), kind=kLoop, calls=%fused_computation.19 | loop fusion | flops 4718592 | bytes 1572868 | tf_op jit(solution)/shard_map/concatenate | solution.py:266
  68.6 0.0 copy-start.2
  68.7 0.2 convolution_convert_fusion.3
  68.9 0.3 fusion.1
  69.2 1.3 %collective-permute-start.15 = (bf16[256,512]{1,0:T(8,128)(2,1)S(1)}, bf16[256,512]{1,0:T(8,128)(2,1)S(1)}, u32[]{:S(2)}, u32[]{:S(2)}) collective-permute-start(bf16[256,512]{1,0:T(8,128)(2,1)S(1)} %fusion.1), channel_id=1, source_target_pairs={{0,2},{2,0},{1,3},{3,1},{4,6},{6,4},{5,7},{7,5},{8,10},{10,8},{9,1... | collective-permute-start | bytes 786440 | tf_op jit(solution)/shard_map/ppermute | solution.py:258
  70.5 0.4 fusion
  71.0 0.3 fusion.3.value
  71.3 44.6 %shard_map.184 = f32[3072,256]{1,0:T(8,128)S(1)} custom-call(bf16[3072,256]{1,0:T(8,128)(2,1)S(1)} %fusion.3.value), custom_call_target="tpu_custom_call" | custom-call | tf_op jit(solution)/shard_map/pallas_call | solution.py:201
  115.9 0.1 fusion.35
  116.0 0.9 pad_maximum_fusion.5
  116.9 0.9 pad_maximum_fusion.4
  117.7 1.4 %fusion.36 = (f32[1024,256]{1,0:T(8,128)}, f32[1024,256]{1,0:T(8,128)}) fusion(f32[3072,256]{1,0:T(8,128)S(1)} %shard_map.184), kind=kLoop, calls=%fused_computation.87 | loop fusion | bytes 4194304 | tf_op jit(solution)/shard_map/slice | solution.py:416
  119.2 0.8 add_convert_fusion
  (39 shorter events, 0.4 us)
Async XLA Ops:
  0.6 17.1 %collective-permute-start.7 = (bf16[256]{0:T(256)(128)(2,1)}, bf16[256]{0:T(256)(128)(2,1)S(1)}, u32[]{:S(2)}, u32[]{:S(2)}) collective-permute-start(bf16[256]{0:T(256)(128)(2,1)} %param.24), channel_id=1, source_target_pairs={{0,2},{2,0},{1,3},{3,1},{4,6},{6,4},{5,7},{7,5},{8,10},{10,8},{9,1... | collective-permute-start | bytes 1544 | tf_op jit(solution)/shard_map/ppermute | solution.py:258
  3.2 6.0 %collective-permute-start = (bf16[256,256]{1,0:T(8,128)(2,1)S(1)}, bf16[256,256]{1,0:T(8,128)(2,1)S(1)}, u32[]{:S(2)}, u32[]{:S(2)}) collective-permute-start(bf16[256,256]{1,0:T(8,128)(2,1)S(1)} %convolution_convert_fusion.5.own_part), channel_id=1, source_target_pairs={{0,1},{1,0},{2,3},{3,2},{4,5},{5,4},{6,7},{7,6},{8,9},{9,8},{10,11... | collective-permute-start | bytes 393224 | tf_op jit(solution)/shard_map/ppermute | solution.py:255
  4.2 27.9 %collective-permute-start.8 = (bf16[256,512]{1,0:T(8,128)(2,1)}, bf16[256,512]{1,0:T(8,128)(2,1)S(1)}, u32[]{:S(2)}, u32[]{:S(2)}) collective-permute-start(bf16[256,512]{1,0:T(8,128)(2,1)} %param.25), channel_id=1, source_target_pairs={{0,2},{2,0},{1,3},{3,1},{4,6},{6,4},{5,7},{7,5},{8,10},{10,8},{9,1... | collective-permute-start | bytes 786440 | tf_op jit(solution)/shard_map/ppermute | solution.py:258
  9.2 1.7 %copy-start = (bf16[2560,512]{1,0:T(8,128)(2,1)S(1)}, bf16[2560,512]{1,0:T(8,128)(2,1)}, u32[]{:S(2)}) copy-start(bf16[2560,512]{1,0:T(8,128)(2,1)} %lat.3) | copy-start | bytes 7864324
  10.9 6.8 %copy-start.5 = (bf16[256,512]{1,0:T(8,128)(2,1)S(1)}, bf16[256,512]{1,0:T(8,128)(2,1)}, u32[]{:S(2)}) copy-start(bf16[256,512]{1,0:T(8,128)(2,1)} %param.27) | copy-start | bytes 786436
  10.9 6.8 %copy-start.8 = (bf16[512]{0:T(512)(128)(2,1)S(1)}, bf16[512]{0:T(512)(128)(2,1)}, u32[]{:S(2)}) copy-start(bf16[512]{0:T(512)(128)(2,1)} %param.26) | copy-start | bytes 3076
  10.9 6.8 %copy-start.4 = (bf16[256,512]{1,0:T(8,128)(2,1)S(1)}, bf16[256,512]{1,0:T(8,128)(2,1)}, u32[]{:S(2)}) copy-start(bf16[256,512]{1,0:T(8,128)(2,1)} %param.22) | copy-start | bytes 786436
  10.9 8.1 %copy-start.9 = (bf16[256]{0:T(256)(128)(2,1)S(1)}, bf16[256]{0:T(256)(128)(2,1)}, u32[]{:S(2)}) copy-start(bf16[256]{0:T(256)(128)(2,1)} %param.24) | copy-start | bytes 1540
  15.4 16.7 %copy-start.7 = (bf16[256,512]{1,0:T(8,128)(2,1)S(1)}, bf16[256,512]{1,0:T(8,128)(2,1)}, u32[]{:S(2)}) copy-start(bf16[256,512]{1,0:T(8,128)(2,1)} %param.25) | copy-start | bytes 786436
  16.2 5.1 %collective-permute-start.1 = (bf16[256,256]{1,0:T(8,128)(2,1)}, bf16[256,256]{1,0:T(8,128)(2,1)S(1)}, u32[]{:S(2)}, u32[]{:S(2)}) collective-permute-start(bf16[256,256]{1,0:T(8,128)(2,1)} %get-tuple-element.36), channel_id=1, source_target_pairs={{0,4},{4,8},{8,12},{12,0},{1,5},{5,9},{9,13},{13,1},{2,6},{6,10},{... | collective-permute-start | bytes 393224 | tf_op jit(solution)/shard_map/ppermute | solution.py:279
  16.2 7.6 %collective-permute-start.3 = (bf16[256,256]{1,0:T(8,128)(2,1)}, bf16[256,256]{1,0:T(8,128)(2,1)S(1)}, u32[]{:S(2)}, u32[]{:S(2)}) collective-permute-start(bf16[256,256]{1,0:T(8,128)(2,1)} %get-tuple-element.37), channel_id=1, source_target_pairs={{0,12},{4,0},{8,4},{12,8},{1,13},{5,1},{9,5},{13,9},{2,14},{6,2},{... | collective-permute-start | bytes 393224 | tf_op jit(solution)/shard_map/ppermute | solution.py:279
  17.7 12.1 %collective-permute-start.2 = (bf16[256,256]{1,0:T(8,128)(2,1)}, bf16[256,256]{1,0:T(8,128)(2,1)}, u32[]{:S(2)}, u32[]{:S(2)}) collective-permute-start(bf16[256,256]{1,0:T(8,128)(2,1)} %get-tuple-element.38), channel_id=1, source_target_pairs={{0,8},{4,12},{8,0},{12,4},{1,9},{5,13},{9,1},{13,5},{2,10},{6,14},... | collective-permute-start | bytes 393224 | tf_op jit(solution)/shard_map/ppermute | solution.py:279
  17.8 14.3 %collective-permute-start.5 = (bf16[256,512]{1,0:T(8,128)(2,1)S(1)}, bf16[256,512]{1,0:T(8,128)(2,1)S(1)}, u32[]{:S(2)}, u32[]{:S(2)}) collective-permute-start(bf16[256,512]{1,0:T(8,128)(2,1)S(1)} %copy-done.4), channel_id=1, source_target_pairs={{0,2},{2,0},{1,3},{3,1},{4,6},{6,4},{5,7},{7,5},{8,10},{10,8},{9,1... | collective-permute-start | bytes 786440 | tf_op jit(solution)/shard_map/ppermute | solution.py:258
  19.1 17.5 %copy-start.6 = (bf16[1024,256]{1,0:T(8,128)(2,1)S(1)}, bf16[1024,256]{1,0:T(8,128)(2,1)}, u32[]{:S(2)}) copy-start(bf16[1024,256]{1,0:T(8,128)(2,1)} %param.23) | copy-start | bytes 1572868
  21.3 15.2 %collective-permute-start.6 = (bf16[1024,256]{1,0:T(8,128)(2,1)}, bf16[1024,256]{1,0:T(8,128)(2,1)S(1)}, u32[]{:S(2)}, u32[]{:S(2)}) collective-permute-start(bf16[1024,256]{1,0:T(8,128)(2,1)} %param.23), channel_id=1, source_target_pairs={{0,2},{2,0},{1,3},{3,1},{4,6},{6,4},{5,7},{7,5},{8,10},{10,8},{9,1... | collective-permute-start | bytes 1572872 | tf_op jit(solution)/shard_map/ppermute | solution.py:258
  30.8 5.7 %collective-permute-start.4 = (bf16[128,256]{1,0:T(8,128)(2,1)S(1)}, bf16[128,256]{1,0:T(8,128)(2,1)S(1)}, u32[]{:S(2)}, u32[]{:S(2)}) collective-permute-start(bf16[128,256]{1,0:T(8,128)(2,1)S(1)} %get-tuple-element.44), channel_id=1, source_target_pairs={{0,2},{2,0},{1,3},{3,1},{4,6},{6,4},{5,7},{7,5},{8,10},{10,8},{9,1... | collective-permute-start | bytes 196616 | tf_op jit(solution)/shard_map/ppermute | solution.py:258
  38.3 10.8 %collective-permute-start.9 = (bf16[128,512]{1,0:T(8,128)(2,1)S(1)}, bf16[128,512]{1,0:T(8,128)(2,1)S(1)}, u32[]{:S(2)}, u32[]{:S(2)}) collective-permute-start(bf16[128,512]{1,0:T(8,128)(2,1)S(1)} %get-tuple-element.19), channel_id=1, source_target_pairs={{0,2},{2,0},{1,3},{3,1},{4,6},{6,4},{5,7},{7,5},{8,10},{10,8},{9,1... | collective-permute-start | bytes 393224 | tf_op jit(solution)/shard_map/ppermute | solution.py:258
  39.6 4.0 %collective-permute-start.10 = (bf16[128,512]{1,0:T(8,128)(2,1)S(1)}, bf16[128,512]{1,0:T(8,128)(2,1)S(1)}, u32[]{:S(2)}, u32[]{:S(2)}) collective-permute-start(bf16[128,512]{1,0:T(8,128)(2,1)S(1)} %get-tuple-element.20), channel_id=1, source_target_pairs={{0,2},{2,0},{1,3},{3,1},{4,6},{6,4},{5,7},{7,5},{8,10},{10,8},{9,1... | collective-permute-start | bytes 393224 | tf_op jit(solution)/shard_map/ppermute | solution.py:258
  39.9 24.9 %collective-permute-start.16 = (bf16[128,1536]{1,0:T(8,128)(2,1)S(1)}, bf16[128,1536]{1,0:T(8,128)(2,1)S(1)}, u32[]{:S(2)}, u32[]{:S(2)}) collective-permute-start(bf16[128,1536]{1,0:T(8,128)(2,1)S(1)} %pad_maximum_fusion.6), channel_id=1, source_target_pairs={{0,2},{2,0},{1,3},{3,1},{4,6},{6,4},{5,7},{7,5},{8,10},{10,8},{9,1... | collective-permute-start | bytes 1179656 | tf_op jit(solution)/shard_map/ppermute | solution.py:258
  44.0 9.3 %copy-start.1 = (bf16[2560,512]{1,0:T(8,128)(2,1)S(1)}, bf16[2560,512]{1,0:T(8,128)(2,1)}, u32[]{:S(2)}) copy-start(bf16[2560,512]{1,0:T(8,128)(2,1)} %lat.3) | copy-start | bytes 7864324
  44.3 5.9 %collective-permute-start.13 = (bf16[256,256]{1,0:T(8,128)(2,1)S(1)}, bf16[256,256]{1,0:T(8,128)(2,1)S(1)}, u32[]{:S(2)}, u32[]{:S(2)}) collective-permute-start(bf16[256,256]{1,0:T(8,128)(2,1)S(1)} %convolution_convert_fusion.4), channel_id=1, source_target_pairs={{0,12},{4,0},{8,4},{12,8},{1,13},{5,1},{9,5},{13,9},{2,14},{6,2},{... | collective-permute-start | bytes 393224 | tf_op jit(solution)/shard_map/ppermute | solution.py:279
  44.8 8.1 %collective-permute-start.12 = (bf16[256,256]{1,0:T(8,128)(2,1)S(1)}, bf16[256,256]{1,0:T(8,128)(2,1)S(1)}, u32[]{:S(2)}, u32[]{:S(2)}) collective-permute-start(bf16[256,256]{1,0:T(8,128)(2,1)S(1)} %convolution_convert_fusion.4), channel_id=1, source_target_pairs={{0,8},{4,12},{8,0},{12,4},{1,9},{5,13},{9,1},{13,5},{2,10},{6,14},... | collective-permute-start | bytes 393224 | tf_op jit(solution)/shard_map/ppermute | solution.py:279
  47.9 5.4 %collective-permute-start.11 = (bf16[256,256]{1,0:T(8,128)(2,1)S(1)}, bf16[256,256]{1,0:T(8,128)(2,1)S(1)}, u32[]{:S(2)}, u32[]{:S(2)}) collective-permute-start(bf16[256,256]{1,0:T(8,128)(2,1)S(1)} %convolution_convert_fusion.4), channel_id=1, source_target_pairs={{0,4},{4,8},{8,12},{12,0},{1,5},{5,9},{9,13},{13,1},{2,6},{6,10},{... | collective-permute-start | bytes 393224 | tf_op jit(solution)/shard_map/ppermute | solution.py:279
  57.3 11.6 %copy-start.3 = (bf16[1024,256]{1,0:T(8,128)(2,1)S(1)}, bf16[1024,256]{1,0:T(8,128)(2,1)}, u32[]{:S(2)}) copy-start(bf16[1024,256]{1,0:T(8,128)(2,1)} %param.20) | copy-start | bytes 1572868
  57.4 11.6 %collective-permute-start.14 = (bf16[256,256]{1,0:T(8,128)(2,1)S(1)}, bf16[256,256]{1,0:T(8,128)(2,1)S(1)}, u32[]{:S(2)}, u32[]{:S(2)}) collective-permute-start(bf16[256,256]{1,0:T(8,128)(2,1)S(1)} %convert_element_type.74), channel_id=1, source_target_pairs={{0,1},{1,0},{2,3},{3,2},{4,5},{5,4},{6,7},{7,6},{8,9},{9,8},{10,11... | collective-permute-start | bytes 393224 | tf_op jit(solution)/shard_map/ppermute | solution.py:255
  68.6 1.9 %copy-start.2 = (bf16[256,512]{1,0:T(8,128)(2,1)S(1)}, bf16[256,512]{1,0:T(8,128)(2,1)}, u32[]{:S(2)}) copy-start(bf16[256,512]{1,0:T(8,128)(2,1)} %param.15) | copy-start | bytes 786436
  69.2 50.0 %collective-permute-start.15 = (bf16[256,512]{1,0:T(8,128)(2,1)S(1)}, bf16[256,512]{1,0:T(8,128)(2,1)S(1)}, u32[]{:S(2)}, u32[]{:S(2)}) collective-permute-start(bf16[256,512]{1,0:T(8,128)(2,1)S(1)} %fusion.1), channel_id=1, source_target_pairs={{0,2},{2,0},{1,3},{3,1},{4,6},{6,4},{5,7},{7,5},{8,10},{10,8},{9,1... | collective-permute-start | bytes 786440 | tf_op jit(solution)/shard_map/ppermute | solution.py:258

commit v2 on v1

v2 whole, which is shorter than its diff:
```python
import functools
import jax
import jax.numpy as jnp
from jax import lax
from jax.experimental import pallas as pl
from jax.experimental.pallas import tpu as pltpu
from jax.sharding import PartitionSpec as P

F32 = jnp.float32
BF16 = jnp.bfloat16
MESH = pl.DeviceIdType.MESH
VMEM_BYTES = 48 * 1024 * 1024


def dot(a, b):
    return jnp.dot(a, b, preferred_element_type=F32)


def dot_t(a, b):
    return lax.dot_general(a, b, (((1,), (1,)), ((), ())), preferred_element_type=F32)


def t_dot(a, b):
    return lax.dot_general(a, b, (((0,), (0,)), ((), ())), preferred_element_type=F32)


def logistic(v):
    return 1.0 / (1.0 + jnp.exp(-v))


def edge_forward_kernel(
    block_rows, per_step, codes, lat, send, slot, own_part, other_part, w_lat, bias, agg, slope, total
):
    step = pl.program_id(0)
    edges = lat.shape[0]
    nodes = own_part.shape[0]

    @pl.when(step == 0)
    def _():
        total[...] = jnp.zeros_like(total)

    places = lax.broadcasted_iota(jnp.int32, (nodes, edges), 0)
    ids = send[0]
    pre = dot(lat[...], w_lat[...]) + bias[...].astype(F32)
    pre += t_dot((places == ids).astype(BF16), own_part[...])
    pre += t_dot((places + nodes == ids).astype(BF16), other_part[...])
    gate = logistic(pre)
    hidden = (pre * gate).astype(BF16)
    slope[...] = (gate * (1.0 + pre * (1.0 - gate))).astype(BF16)
    rows = lax.broadcasted_iota(jnp.int32, (block_rows, block_rows), 0)
    for j in range(per_step):
        at = slice(j * block_rows, (j + 1) * block_rows)
        pick = (rows == slot[0, :, at]).astype(BF16)
        to = pl.ds(pl.multiple_of(codes[step * per_step + j] * block_rows, block_rows), block_rows)
        total[to, :] += dot(pick, hidden[at])

    @pl.when(step == pl.num_programs(0) - 1)
    def _():
        agg[...] = total[...].astype(BF16)


def core_kernel(regions, hids, blocks, per_step, *refs):
    refs = list(refs)

    def take(count):
        got = refs[:count]
        del refs[:count]
        return got

    agg, nodes, cot, gain, w_send, edge_hbm, slope_hbm, send, cell = take(9)
    weo, wni, bn, wno = take(hids), take(hids), take(hids), take(hids)
    new_o, grad_nodes_o, gei_o, geo_o, gni_o, gno_o = take(6)
    edge_v, slope_v, from_region, gk, agg_mine, hidden, gnp = take(7)
    gg_all, gathered_all, gu_all, hid_all, gnp_all, new_all = take(6)
    gs_all, sent_part, own_part, other_part, lat_part, sub_part, node_part, node_parts = take(8)
    stack1, from_sub1, shared1, half1, arrived1, piece1, whole1 = take(7)
    stack2, from_sub2, shared2, half2, arrived2, piece2, whole2, result = take(8)
    local_sem, region_sems, hid_sems, sub_sems, red1_sems, red2_sems = take(6)

    me = lax.axis_index("region")
    hid = lax.axis_index("hid")
    sub = lax.axis_index("sub")
    other = 1 - sub
    count, latent = nodes.shape
    width = gk.shape[1]
    share = count // hids
    block_rows = edge_v.shape[0] // blocks
    span = per_step * block_rows

    fetch = [
        pltpu.make_async_copy(edge_hbm, edge_v, local_sem.at[0]),
        pltpu.make_async_copy(slope_hbm, slope_v, local_sem.at[1]),
    ]
    for copy in fetch:
        copy.start()
    barrier = pltpu.get_barrier_semaphore()
    pl.semaphore_signal(barrier, inc=1, device_id={"sub": other}, device_id_type=MESH)
    for j in range(1, regions):
        pl.semaphore_signal(
            barrier, inc=1, device_id={"region": lax.rem(me + j, regions)}, device_id_type=MESH
        )
    for j in range(1, hids):
        pl.semaphore_signal(
            barrier, inc=1, device_id={"hid": lax.rem(hid + j, hids)}, device_id_type=MESH
        )
    pl.semaphore_wait(barrier, regions + hids - 1)
    started = []

    def push(source, target, sems, index, device):
        copy = pltpu.make_async_remote_copy(
            source, target, sems.at[0, index], sems.at[1, index],
            device_id=device, device_id_type=MESH,
        )
        copy.start()
        started.append(copy)
        return copy

    def to_region(j):
        return {"region": lax.rem(me + j, regions)}

    def to_hid(j):
        return {"hid": lax.rem(hid + j, hids)}

    def rows(index, size):
        return pl.ds(pl.multiple_of(index * size, 16), size)

    def hid_push(kind, source, target):
        return [
            push(source(j), target(j), hid_sems, kind * hids + j, to_hid(j))
            for j in range(1, hids)
        ]

    def arrive(copies):
        for copy in copies:
            copy.wait_recv()

    copies = [
        push(agg.at[j], from_region.at[j], region_sems, j, to_region(j)) for j in range(1, regions)
    ]
    my_rows = rows(hid, share)
    lat = nodes[my_rows, :]
    pre_lat = [dot(lat, wni[j][:latent, :]) + bn[j][...].astype(F32) for j in range(hids)]
    total = agg[0].astype(F32)
    for j in range(1, regions):
        copies[j - 1].wait_recv()
        total = total + from_region[j].astype(F32)
    gk[...] = total.astype(BF16)
    copies = hid_push(
        0, lambda j: gk.at[rows(lax.rem(hid + j, hids), share), :], lambda j: agg_mine.at[j]
    )
    agg_own = gk[my_rows, :]
    gathered = dot(agg_own, weo[0][...])
    for j in range(1, hids):
        copies[j - 1].wait_recv()
        gathered = gathered + dot(agg_mine[j], weo[j][...])
    gathered = gathered.astype(BF16)
    gathered_all[my_rows, :] = gathered

    slopes = []
    update = None
    for j in range(hids):
        pre = pre_lat[j] + dot(gathered, wni[j][latent:, :])
        gate = logistic(pre)
        units = (pre * gate).astype(BF16)
        hidden[j] = units
        slopes.append(gate * (1.0 + pre * (1.0 - gate)))
        term = dot(units, wno[j][...])
        update = term if update is None else update + term
    scale = gain[...].astype(F32)
    centred = update - jnp.mean(update, axis=-1, keepdims=True)
    inv = lax.rsqrt(jnp.mean(centred * centred, axis=-1, keepdims=True) + 1e-05)
    unit = centred * inv
    cot_gain = cot[my_rows, :].astype(F32) * scale
    grad = cot_gain - jnp.mean(cot_gain, axis=-1, keepdims=True)
    grad = (grad - unit * jnp.mean(cot_gain * unit, axis=-1, keepdims=True)) * inv
    grad = grad.astype(BF16)
    gu_all[my_rows, :] = grad
    gg = None
    for j in range(hids):
        units = (dot_t(grad, wno[j][...]) * slopes[j]).astype(BF16)
        gnp[j] = units
        term = dot_t(units, wni[j][latent:, :])
        gg = term if gg is None else gg + term
    gg_all[my_rows, :] = gg.astype(BF16)
    gg_copies = hid_push(1, lambda j: gg_all.at[my_rows, :], lambda j: gg_all.at[my_rows, :])
    new_all[my_rows, :] = (lat.astype(F32) + unit * scale).astype(BF16)
    hid_all[my_rows, :] = hidden[0]
    gnp_all[my_rows, :] = gnp[0]
    back = lambda j: (hids - j) % hids
    pack = hid_push(2, lambda j: gnp.at[back(j)], lambda j: gnp_all.at[my_rows, :])
    pack += hid_push(3, lambda j: hidden.at[back(j)], lambda j: hid_all.at[my_rows, :])
    pack += hid_push(4, lambda j: gathered_all.at[my_rows, :], lambda j: gathered_all.at[my_rows, :])
    pack += hid_push(5, lambda j: gu_all.at[my_rows, :], lambda j: gu_all.at[my_rows, :])
    new_copies = hid_push(6, lambda j: new_all.at[my_rows, :], lambda j: new_all.at[my_rows, :])
    arrive(gg_copies)
    gs_all[:count, :] = dot_t(gg_all[...], weo[0][...]).astype(BF16)
    gs_copies = [
        push(
            gs_all.at[pl.ds(0, count), :], gs_all.at[pl.ds(j * count, count), :],
            region_sems, regions + j, to_region(j),
        )
        for j in range(1, regions)
    ]

    def reducer(stack, from_sub, shared, half_sum, arrived, piece, whole, sems, base):
        half = half_sum.shape[0]
        chunk = half // regions
        held = {}

        def begin():
            held["sub"] = push(
                stack.at[rows(other, half), :], from_sub, sems, 0, {"sub": other}
            )

        def scatter():
            held["sub"].wait_recv()
            half_sum[...] = (
                stack[rows(sub, half), :].astype(F32) + from_sub[...].astype(F32)
            ).astype(BF16)
            held["rs"] = [
                push(
                    half_sum.at[rows(lax.rem(me + j, regions), chunk), :], arrived.at[j],
                    sems, j, to_region(j),
                )
                for j in range(1, regions)
            ]

        def give(source, j):
            target = shared.at[pl.ds(j * chunk, chunk), :]
            held["share"].append(
                push(source, target, sems, 2 * regions + j, {"sub": other})
            )
            origin = lax.rem(me - j + regions, regions)
            result[rows(base // chunk + sub * regions + origin, chunk), :] = source[...].astype(F32)

        def gather():
            total = half_sum[rows(me, chunk), :].astype(F32)
            for j in range(1, regions):
                held["rs"][j - 1].wait_recv()
                total = total + arrived[j].astype(F32)
            piece[...] = total.astype(BF16)
            held["ag"] = [
                push(piece, whole.at[j], sems, regions + j, to_region(j))
                for j in range(1, regions)
            ]
            held["share"] = []
            give(piece, 0)

        def spread():
            for j in range(1, regions):
                held["ag"][j - 1].wait_recv()
                give(whole.at[j], j)

        def finish():
            for j in range(regions):
                held["share"][j].wait_recv()
                origin = lax.rem(me - j + regions, regions)
                result[rows(base // chunk + other * regions + origin, chunk), :] = shared[
                    j * chunk:(j + 1) * chunk, :
                ].astype(F32)

        return begin, scatter, gather, spread, finish

    begin1, scatter1, gather1, spread1, finish1 = reducer(
        stack1, from_sub1, shared1, half1, arrived1, piece1, whole1, red1_sems, 0
    )
    begin2, scatter2, gather2, spread2, finish2 = reducer(
        stack2, from_sub2, shared2, half2, arrived2, piece2, whole2, red2_sems, 4 * latent
    )

    edge_out = t_dot(gk[...], gg_all[...]).astype(BF16)
    arrive(pack)
    units = gnp_all[...]
    stack1[:latent, :] = t_dot(nodes[...], units).astype(BF16)
    stack1[latent:2 * latent, :] = t_dot(gathered_all[...], units).astype(BF16)
    node_out = t_dot(hid_all[...], gu_all[...]).astype(BF16)
    for at in range(0, latent, width):
        stack1[2 * latent + at:2 * latent + at + width, :] = node_out[:, at:at + width]
        stack1[3 * latent + at:3 * latent + at + width, :] = edge_out[:, at:at + width]
    begin1()
    cat = None
    for j in range(hids):
        term = dot_t(gnp[j], wni[j][:latent, :])
        cat = term if cat is None else cat + term
    sent_part[...] = jnp.zeros_like(sent_part)
    sent_part[my_rows, :] = cat
    arrive(new_copies)
    new_o[...] = new_all[...]
    scatter1()

    for copy in fetch:
        copy.wait()
    lat_part[...] = jnp.zeros_like(lat_part)
    own_part[...] = jnp.zeros_like(own_part)
    other_part[...] = jnp.zeros_like(other_part)
    arrive(gs_copies)
    places = lax.broadcasted_iota(jnp.int32, (count, span), 0)
    cells = lax.broadcasted_iota(jnp.int32, (gs_all.shape[0], span), 0)

    def edge_step(step, carry):
        ids = send[step]
        at = pl.ds(pl.multiple_of(step * span, 16), span)
        grad_hidden = t_dot((cells == cell[step]).astype(BF16), gs_all[...])
        grad_pre = (grad_hidden * slope_v[at, :].astype(F32)).astype(BF16)
        lat_part[...] += t_dot(edge_v[at, :], grad_pre)
        own_part[...] += dot((places == ids).astype(BF16), grad_pre)
        other_part[...] += dot((places + count == ids).astype(BF16), grad_pre)
        return carry

    lax.fori_loop(0, blocks // per_step, edge_step, 0)
    sub_part[0] = other_part[...].astype(BF16)
    sub_copy = push(sub_part.at[0], sub_part.at[1], sub_sems, 0, {"sub": other})
    stack2[:latent, :] = lat_part[...].astype(BF16)
    gather1()
    sub_copy.wait_recv()
    grad_send = (own_part[...] + sub_part[1].astype(F32)).astype(BF16)
    stack2[latent:, :] = t_dot(nodes[...], grad_send).astype(BF16)
    begin2()
    node_part[...] = (sent_part[...] + dot_t(grad_send, w_send[...])).astype(BF16)
    part_copies = hid_push(7, lambda j: node_part, lambda j: node_parts.at[j])
    scatter2()
    spread1()
    gather2()
    total = cot[...].astype(F32) + node_part[...].astype(F32)
    for j in range(1, hids):
        part_copies[j - 1].wait_recv()
        total = total + node_parts[j].astype(F32)
    grad_nodes_o[...] = total.astype(BF16)
    finish1()
    gni_o[...] = result[:2 * latent, :]
    for at in range(0, latent, width):
        gno_o[:, at:at + width] = result[2 * latent + at:2 * latent + at + width, :]
        geo_o[:, at:at + width] = result[3 * latent + at:3 * latent + at + width, :]
    spread2()
    finish2()
    gei_o[...] = result[4 * latent:, :]
    for copy in started:
        copy.wait_send()


def on_device(
    edge_lat,
    node_lat,
    senders,
    recv_slots,
    owners,
    targets,
    w_edge_in,
    b_edge,
    w_edge_out,
    w_node_in,
    b_node,
    w_node_out,
    norm_gain,
    cotangent,
):
    regions = lax.axis_size("region")
    me = lax.axis_index("region")
    sub = lax.axis_index("sub")
    blocks = owners.shape[0]
    edges = edge_lat.shape[0]
    block_rows = edges // blocks
    node_rows, latent = node_lat.shape
    width = w_edge_in.shape[1]
    recv_blocks = node_rows // block_rows
    hids = lax.axis_size("hid")
    share = node_rows // hids
    per_step = 4 if blocks % 4 == 0 else 1
    steps = blocks // per_step
    span = per_step * block_rows

    def swap(value, axis):
        return lax.ppermute(value, axis, [(0, 1), (1, 0)])

    def hid_shift(value, by):
        return lax.ppermute(value, "hid", [(i, (i + by) % hids) for i in range(hids)])

    def hid_all(value):
        return [value] + [hid_shift(value, j) for j in range(1, hids)]

    weo = hid_all(w_edge_out)
    wni = hid_all(w_node_in)
    wno = hid_all(w_node_out)
    bn = hid_all(b_node[None])

    own_part = jnp.dot(node_lat, w_edge_in[latent:], preferred_element_type=F32).astype(BF16)
    other_part = swap(own_part, "sub")

    owner = owners[:, 0]
    ahead = lax.rem(owner - me + regions, regions) * recv_blocks + targets
    behind = lax.rem(me - owner + regions, regions) * recv_blocks + targets
    cell = behind[:, None] * block_rows + recv_slots.reshape(blocks, block_rows)
    send_rows = jnp.bitwise_xor(senders // node_rows, sub) * node_rows + senders % node_rows
    send_rows = send_rows.reshape(steps, 1, span)
    slots = recv_slots.reshape(steps, 1, span)
    cell = cell.reshape(steps, 1, span)
    whole = lambda *shape: pl.BlockSpec(shape, lambda i, c: (0,) * len(shape))
    tile = lambda cols: pl.BlockSpec((span, cols), lambda i, c: (i, 0))
    ids = pl.BlockSpec((1, 1, span), lambda i, c: (i, 0, 0))
    params = pltpu.CompilerParams(vmem_limit_bytes=VMEM_BYTES)
    agg_rows = regions * node_rows

    agg, slope = pl.pallas_call(
        functools.partial(edge_forward_kernel, block_rows, per_step),
        out_shape=(
            jax.ShapeDtypeStruct((agg_rows, width), BF16),
            jax.ShapeDtypeStruct((edges, width), BF16),
        ),
        grid_spec=pltpu.PrefetchScalarGridSpec(
            num_scalar_prefetch=1,
            grid=(steps,),
            in_specs=[
                tile(latent), ids, ids, whole(node_rows, width), whole(node_rows, width),
                whole(latent, width), whole(1, width),
            ],
            out_specs=[whole(agg_rows, width), tile(width)],
            scratch_shapes=[pltpu.VMEM((agg_rows, width), F32)],
        ),
        compiler_params=params,
    )(ahead, edge_lat, send_rows, slots, own_part, other_part, w_edge_in[:latent], b_edge[None])

    agg = agg.reshape(regions, node_rows, width)
    vmem = pl.BlockSpec(memory_space=pltpu.VMEM)
    hbm = pl.BlockSpec(memory_space=pl.ANY)
    dma = pltpu.SemaphoreType.DMA
    low = lambda *shape: pltpu.VMEM(shape, BF16)
    high = lambda *shape: pltpu.VMEM(shape, F32)

    def reduce_scratch(height):
        half = height // 2
        chunk = half // regions
        return [
            low(height, width), low(half, width), low(half, width), low(half, width),
            low(regions, chunk, width), low(chunk, width), low(regions, chunk, width),
        ]

    return pl.pallas_call(
        functools.partial(core_kernel, regions, hids, blocks, per_step),
        out_shape=(
            jax.ShapeDtypeStruct((node_rows, latent), BF16),
            jax.ShapeDtypeStruct((node_rows, latent), BF16),
            jax.ShapeDtypeStruct((2 * latent, width), F32),
            jax.ShapeDtypeStruct((width, latent), F32),
            jax.ShapeDtypeStruct((2 * latent, width), F32),
            jax.ShapeDtypeStruct((width, latent), F32),
        ),
        in_specs=[vmem] * 5 + [hbm] * 2 + [vmem] * (2 + 4 * hids),
        out_specs=(vmem,) * 6,
        scratch_shapes=[
            low(edges, latent), low(edges, width), low(regions, node_rows, width),
            low(node_rows, width), low(hids, share, width), low(hids, share, width),
            low(hids, share, width),
            low(node_rows, latent), low(node_rows, latent), low(node_rows, latent),
            low(node_rows, width), low(node_rows, width), low(node_rows, latent),
            low(agg_rows, width), high(node_rows, latent), high(node_rows, width),
            high(node_rows, width), high(latent, width), low(2, node_rows, width),
            low(node_rows, latent), low(hids, node_rows, latent),
            *reduce_scratch(4 * latent),
            *reduce_scratch(2 * latent),
            high(6 * latent, width),
            dma((2,)), dma((2, 2 * regions)), dma((2, 8 * hids)), dma((2, 1)),
            dma((2, 3 * regions)), dma((2, 3 * regions)),
        ],
        compiler_params=pltpu.CompilerParams(
            collective_id=1, has_side_effects=True, vmem_limit_bytes=VMEM_BYTES
        ),
    )(
        agg, node_lat, cotangent, norm_gain[None], w_edge_in[latent:], edge_lat, slope,
        send_rows, cell, *weo, *wni, *bn, *wno,
    )


def solution(mesh):
    placed = (
        P(("group", "region", "sub"), None),
        P(("group", "region", "sub"), None),
        P(("group", "region", "sub")),
        P(("group", "region", "sub")),
        P(("group", "region", "sub"), None),
        P(("group", "region", "sub")),
        P(None, "hid"),
        P("hid"),
        P("hid", None),
        P(None, "hid"),
        P("hid"),
        P("hid", None),
        P(),
        P(("group", "region", "sub"), None),
    )
    return jax.shard_map(
        on_device,
        mesh=mesh,
        in_specs=placed,
        out_specs=(
            P(("group", "region", "sub"), None),
            P(("group", "region", "sub"), None),
            P("group", "hid"),
            P(("group", "hid"), None),
            P("group", "hid"),
            P(("group", "hid"), None),
        ),
        check_vma=False,
    )
```

time: 120 us -> 110 us (0.917); the launches traced: 120 us -> 108 us
  Pallas kernels: 54.7 us -> 77.7 us
  starting transfers between devices: 23.9 us -> 3.98 us
  other arithmetic: 10.6 us -> 1.43 us
  waiting for transfers between devices: 19.3 us -> 11.2 us
  local copies, waits for them, and re-layouts: 7.5 us -> 11.8 us
  matrix products: 2.89 us -> 1.25 us
    pallas_call x3 -> x1, Pallas kernels: 50.2 us -> 73.3 us  [on_device(): pl.pallas_call(functools.partial(core_kernel, regions, hids, blocks, per_...]
    ppermute x6 -> x0, waiting for transfers between devices: 12.5 us -> none  [shift(): lax.ppermute(value, 'region', [(i, (i + by) % regions) for i in range(reg...]
    ppermute x2 -> x1, starting transfers between devices: 8.45 us -> 1.02 us  [swap(): return lax.ppermute(value, axis, [(0, 1), (1, 0)])]
    concatenate x12 -> x0, other arithmetic: 7.4 us -> none  [the longest x3 5.45 us: ordered(): doubled = jnp.concatenate(descending + descending[:-1], axis=0)]
    ppermute x9 -> x4, starting transfers between devices: 9.44 us -> 2.96 us  [hid_shift(): lax.ppermute(value, 'hid', [(i, (i + by) % hids) for i in range(hids)])]
    ppermute x6 -> x0, starting transfers between devices: 6 us -> none  [shift(): lax.ppermute(value, 'region', [(i, (i + by) % regions) for i in range(reg...]
    unnamed x24 -> x22, local copies, waits for them, and re-layouts: 1.83 us -> 7.76 us
    ppermute x9 -> x4, waiting for transfers between devices: 6.73 us -> 11.2 us  [hid_shift(): lax.ppermute(value, 'hid', [(i, (i + by) % hids) for i in range(hids)])]
  transfers between devices with their start and end apart: 17 -> 5, of which waited for: 7 -> 1; matrix products, arithmetic and copies ran while one was open for 15% -> 6% of each run, Pallas kernels for 44% -> 4%
where the time goes in v2:
time: 110 us; the launch traced here: 108 us
  Pallas kernels  77.7 us (71%)
  local copies, waits for them, and re-layouts  11.8 us (11%)
  waiting for transfers between devices  11.2 us (10%)
  starting transfers between devices  3.98 us (4%)
  other arithmetic  1.43 us (1%)
  matrix products  1.25 us (1%)
    pallas_call x1, Pallas kernels, on_device(): pl.pallas_call(functools.partial(core_kernel, regions, hids, blocks, per_...  73.3 us
    ppermute x4, waiting for transfers between devices, hid_shift(): lax.ppermute(value, 'hid', [(i, (i + by) % hids) for i in range(hids)])  11.2 us
    unnamed x22, local copies, waits for them, and re-layouts  7.76 us
    pallas_call x1, Pallas kernels, on_device(): pl.pallas_call(functools.partial(edge_forward_kernel, block_rows, per_ste...  4.46 us
    ppermute x4, starting transfers between devices, hid_shift(): lax.ppermute(value, 'hid', [(i, (i + by) % hids) for i in range(hids)])  2.96 us
  transfers between devices with their start and end apart: 5, of which 1 were waited for; matrix products, arithmetic and copies ran while one was open for 6% of the time, Pallas kernels for 4%

profile of v2, /device:TPU:25, one launch (start us, length us, event | category | flops | bytes accessed | tf_op | source)
XLA Modules:
  0.0 108.2 jit_solution(14297677141562632143)
XLA Ops:
  0.6 0.0 copy-start.2
  0.6 0.0 copy-start.5
  0.7 0.0 copy-start.6
  0.7 0.0 copy-start.3
  0.7 0.0 copy-start.4
  0.7 0.8 broadcast_in_dim.12.refs_13_
  1.5 1.2 %collective-permute-start.3 = (bf16[1,256]{1,0:T(2,128)(2,1)S(1)}, bf16[1,256]{1,0:T(2,128)(2,1)S(1)}, u32[]{:S(2)}, u32[]{:S(2)}) collective-permute-start(bf16[1,256]{1,0:T(2,128)(2,1)S(1)} %broadcast_in_dim.12.refs_13_), channel_id=1, source_target_pairs={{0,2},{2,0},{1,3},{3,1},{4,6},{6,4},{5,7},{7,5},{8,10},{10,8},{9,1... | collective-permute-start | bytes 1544 | tf_op jit(solution)/shard_map/ppermute | solution.py:376
  2.7 1.3 %convolution_convert_fusion.own_part = bf16[256,256]{1,0:T(8,128)(2,1)S(1)} fusion(bf16[256,512]{1,0:T(8,128)(2,1)} %refs_1_.1, bf16[1024,256]{1,0:T(8,128)(2,1)} %param.20), kind=kOutput, calls=%fused_computation | convolution fusion | flops 67174400 | bytes 655360 | tf_op jit(solution)/shard_map/dot_general | solution.py:386
  3.9 1.0 collective-permute-start
  5.0 0.3 collective-permute-start.1
  5.2 1.2 %collective-permute-start.4 = (bf16[256,512]{1,0:T(8,128)(2,1)}, bf16[256,512]{1,0:T(8,128)(2,1)S(1)}, u32[]{:S(2)}, u32[]{:S(2)}) collective-permute-start(bf16[256,512]{1,0:T(8,128)(2,1)} %refs_15_.1), channel_id=1, source_target_pairs={{0,2},{2,0},{1,3},{3,1},{4,6},{6,4},{5,7},{7,5},{8,10},{10,8},{9,1... | collective-permute-start | bytes 786440 | tf_op jit(solution)/shard_map/ppermute | solution.py:376
  6.4 0.3 collective-permute-start.2
  6.7 1.1 fusion.15
  7.8 0.7 fusion.13
  8.5 0.7 broadcast_in_dim.10.bias
  9.1 0.7 broadcast_in_dim.11.refs_3_
  9.8 0.1 add.55
  9.9 0.7 fusion.2
  10.6 0.7 reshape.58.slot
  11.3 0.1 add.56
  11.4 0.0 collective-permute-done.other_part
  11.4 0.0 copy-start
  11.5 1.7 %copy-done = bf16[2560,512]{1,0:T(8,128)(2,1)S(1)} copy-done((bf16[2560,512]{1,0:T(8,128)(2,1)S(1)}, bf16[2560,512]{1,0:T(8,128)(2,1)}, u32[]{:S(2)}) %copy-start) | copy-done | bytes 2621464
  13.2 4.5 %shard_map.181 = (bf16[1024,256]{1,0:T(8,128)(2,1)S(1)}, bf16[2560,256]{1,0:T(8,128)(2,1)S(1)}) custom-call(s32[20]{0:T(128)S(1)} %get-tuple-element.13.codes, bf16[2560,512]{1,0:T(8,128)(2,1)S(1)} %copy-done, s32[5,1,512]{2,1,0:T(1,128)S(1)} %reshape.57.send.refs_7_, s32[5,1,512]{2,1,0:T(1,128)S(1)} %reshape.58.slot, ...), custom_call_target="tpu_custom_call" | custom-call | tf_op jit(solution)/shard_map/pallas_call | solution.py:403
  17.7 0.0 copy-start.1
  17.7 1.1 copy-done.1
  18.7 0.0 collective-permute-done.3.refs_14_
  18.7 0.0 collective-permute-done.1.refs_10_
  18.7 0.0 collective-permute-done.4.refs_16_
  18.7 11.2 %collective-permute-done.2.refs_12_ = bf16[1024,256]{1,0:T(8,128)(2,1)S(1)} collective-permute-done((bf16[1024,256]{1,0:T(8,128)(2,1)}, bf16[1024,256]{1,0:T(8,128)(2,1)S(1)}, u32[]{:S(2)}, u32[]{:S(2)}) %collective-permute-start.2) | collective-permute-done | bytes 524320 | tf_op jit(solution)/shard_map/ppermute | solution.py:376
  29.9 0.0 copy-done.2
  29.9 0.0 copy-done.5
  29.9 0.0 copy-done.6
  29.9 0.0 copy-done.3
  29.9 0.0 copy-done.4
  29.9 73.3 %shard_map.182 = (bf16[256,512]{1,0:T(8,128)(2,1)S(1)}, bf16[256,512]{1,0:T(8,128)(2,1)S(1)}, f32[1024,256]{1,0:T(8,128)S(1)}, f32[256,512]{1,0:T(8,128)S(1)}, f...) custom-call(bf16[4,256,256]{2,1,0:T(8,128)(2,1)S(1)} %bitcast.9, bf16[256,512]{1,0:T(8,128)(2,1)S(1)} %copy-done.2, ...), custom_call_target="tpu_custom_call" | custom-call | tf_op jit(solution)/shard_map/pallas_call | solution.py:437
  103.2 0.0 copy-start.7
  103.2 0.7 copy.26
  103.9 0.7 copy.27
  104.6 1.0 copy.28
  105.6 0.8 copy.29
  106.4 0.0 copy-done.7
  106.4 1.0 copy.30
  107.4 0.8 copy.31
  (2 shorter events, 0.0 us)
Async XLA Ops:
  0.6 29.3 %copy-start.2 = (bf16[256,512]{1,0:T(8,128)(2,1)S(1)}, bf16[256,512]{1,0:T(8,128)(2,1)}, u32[]{:S(2)}) copy-start(bf16[256,512]{1,0:T(8,128)(2,1)} %refs_1_.1) | copy-start | bytes 786436
  0.6 29.3 %copy-start.5 = (bf16[256,512]{1,0:T(8,128)(2,1)S(1)}, bf16[256,512]{1,0:T(8,128)(2,1)}, u32[]{:S(2)}) copy-start(bf16[256,512]{1,0:T(8,128)(2,1)} %refs_9_.1) | copy-start | bytes 786436
  0.7 29.3 %copy-start.6 = (bf16[256,512]{1,0:T(8,128)(2,1)S(1)}, bf16[256,512]{1,0:T(8,128)(2,1)}, u32[]{:S(2)}) copy-start(bf16[256,512]{1,0:T(8,128)(2,1)} %refs_15_.1) | copy-start | bytes 786436
  0.7 29.2 %copy-start.3 = (bf16[1024,256]{1,0:T(8,128)(2,1)S(1)}, bf16[1024,256]{1,0:T(8,128)(2,1)}, u32[]{:S(2)}) copy-start(bf16[1024,256]{1,0:T(8,128)(2,1)} %refs_11_.1) | copy-start | bytes 1572868
  0.7 29.2 %copy-start.4 = (bf16[256,512]{1,0:T(8,128)(2,1)S(1)}, bf16[256,512]{1,0:T(8,128)(2,1)}, u32[]{:S(2)}) copy-start(bf16[256,512]{1,0:T(8,128)(2,1)} %refs_2_.1) | copy-start | bytes 786436
  1.5 17.3 %collective-permute-start.3 = (bf16[1,256]{1,0:T(2,128)(2,1)S(1)}, bf16[1,256]{1,0:T(2,128)(2,1)S(1)}, u32[]{:S(2)}, u32[]{:S(2)}) collective-permute-start(bf16[1,256]{1,0:T(2,128)(2,1)S(1)} %broadcast_in_dim.12.refs_13_), channel_id=1, source_target_pairs={{0,2},{2,0},{1,3},{3,1},{4,6},{6,4},{5,7},{7,5},{8,10},{10,8},{9,1... | collective-permute-start | bytes 1544 | tf_op jit(solution)/shard_map/ppermute | solution.py:376
  3.9 7.5 %collective-permute-start = (bf16[256,256]{1,0:T(8,128)(2,1)S(1)}, bf16[256,256]{1,0:T(8,128)(2,1)S(1)}, u32[]{:S(2)}, u32[]{:S(2)}) collective-permute-start(bf16[256,256]{1,0:T(8,128)(2,1)S(1)} %convolution_convert_fusion.own_part), channel_id=1, source_target_pairs={{0,1},{1,0},{2,3},{3,2},{4,5},{5,4},{6,7},{7,6},{8,9},{9,8},{10,11... | collective-permute-start | bytes 393224 | tf_op jit(solution)/shard_map/ppermute | solution.py:373
  5.0 13.8 %collective-permute-start.1 = (bf16[256,512]{1,0:T(8,128)(2,1)}, bf16[256,512]{1,0:T(8,128)(2,1)S(1)}, u32[]{:S(2)}, u32[]{:S(2)}) collective-permute-start(bf16[256,512]{1,0:T(8,128)(2,1)} %refs_9_.1), channel_id=1, source_target_pairs={{0,2},{2,0},{1,3},{3,1},{4,6},{6,4},{5,7},{7,5},{8,10},{10,8},{9,1... | collective-permute-start | bytes 786440 | tf_op jit(solution)/shard_map/ppermute | solution.py:376
  5.2 13.5 %collective-permute-start.4 = (bf16[256,512]{1,0:T(8,128)(2,1)}, bf16[256,512]{1,0:T(8,128)(2,1)S(1)}, u32[]{:S(2)}, u32[]{:S(2)}) collective-permute-start(bf16[256,512]{1,0:T(8,128)(2,1)} %refs_15_.1), channel_id=1, source_target_pairs={{0,2},{2,0},{1,3},{3,1},{4,6},{6,4},{5,7},{7,5},{8,10},{10,8},{9,1... | collective-permute-start | bytes 786440 | tf_op jit(solution)/shard_map/ppermute | solution.py:376
  6.4 23.5 %collective-permute-start.2 = (bf16[1024,256]{1,0:T(8,128)(2,1)}, bf16[1024,256]{1,0:T(8,128)(2,1)S(1)}, u32[]{:S(2)}, u32[]{:S(2)}) collective-permute-start(bf16[1024,256]{1,0:T(8,128)(2,1)} %refs_11_.1), channel_id=1, source_target_pairs={{0,2},{2,0},{1,3},{3,1},{4,6},{6,4},{5,7},{7,5},{8,10},{10,8},{9,1... | collective-permute-start | bytes 1572872 | tf_op jit(solution)/shard_map/ppermute | solution.py:376
  11.4 1.7 %copy-start = (bf16[2560,512]{1,0:T(8,128)(2,1)S(1)}, bf16[2560,512]{1,0:T(8,128)(2,1)}, u32[]{:S(2)}) copy-start(bf16[2560,512]{1,0:T(8,128)(2,1)} %refs_5_.1) | copy-start | bytes 7864324
  17.7 1.1 copy-start.1
  103.2 3.2 %copy-start.7 = (f32[1024,256]{1,0:T(8,128)S(1)}, f32[1024,256]{1,0:T(8,128)}, u32[]{:S(2)}) copy-start(f32[1024,256]{1,0:T(8,128)} %get-tuple-element.24) | copy-start | bytes 3145732

commit v3 on v2

--- a/solution.py
+++ b/solution.py
@@ -68,14 +68,15 @@
         return got
 
     agg, nodes, cot, gain, w_send, edge_hbm, slope_hbm, send, cell = take(9)
-    weo, wni, bn, wno = take(hids), take(hids), take(hids), take(hids)
+    weo, wni, bn, wno = take(hids), take(1), take(hids), take(hids)
     new_o, grad_nodes_o, gei_o, geo_o, gni_o, gno_o = take(6)
     edge_v, slope_v, from_region, gk, agg_mine, hidden, gnp = take(7)
     gg_all, gathered_all, gu_all, hid_all, gnp_all, new_all = take(6)
     gs_all, sent_part, own_part, other_part, lat_part, sub_part, node_part, node_parts = take(8)
     stack1, from_sub1, shared1, half1, arrived1, piece1, whole1 = take(7)
     stack2, from_sub2, shared2, half2, arrived2, piece2, whole2, result = take(8)
-    local_sem, region_sems, hid_sems, sub_sems, red1_sems, red2_sems = take(6)
+    wni_all, local_sem, region_sems, hid_sems, sub_sems, red1_sems, red2_sems = take(7)
+    wni += [wni_all.at[j] for j in range(1, hids)]
 
     me = lax.axis_index("region")
     hid = lax.axis_index("hid")
@@ -139,7 +140,7 @@
     ]
     my_rows = rows(hid, share)
     lat = nodes[my_rows, :]
-    pre_lat = [dot(lat, wni[j][:latent, :]) + bn[j][...].astype(F32) for j in range(hids)]
+    weight_copies = hid_push(8, lambda j: wni[0], lambda j: wni_all.at[j])
     total = agg[0].astype(F32)
     for j in range(1, regions):
         copies[j - 1].wait_recv()
@@ -156,6 +157,8 @@
     gathered = gathered.astype(BF16)
     gathered_all[my_rows, :] = gathered
 
+    arrive(weight_copies)
+    pre_lat = [dot(lat, wni[j][:latent, :]) + bn[j][...].astype(F32) for j in range(hids)]
     slopes = []
     update = None
     for j in range(hids):
@@ -379,7 +382,6 @@
         return [value] + [hid_shift(value, j) for j in range(1, hids)]
 
     weo = hid_all(w_edge_out)
-    wni = hid_all(w_node_in)
     wno = hid_all(w_node_out)
     bn = hid_all(b_node[None])
 
@@ -444,7 +446,7 @@
             jax.ShapeDtypeStruct((2 * latent, width), F32),
             jax.ShapeDtypeStruct((width, latent), F32),
         ),
-        in_specs=[vmem] * 5 + [hbm] * 2 + [vmem] * (2 + 4 * hids),
+        in_specs=[vmem] * 5 + [hbm] * 2 + [vmem] * (3 + 3 * hids),
         out_specs=(vmem,) * 6,
         scratch_shapes=[
             low(edges, latent), low(edges, width), low(regions, node_rows, width),
@@ -458,7 +460,8 @@
             *reduce_scratch(4 * latent),
             *reduce_scratch(2 * latent),
             high(6 * latent, width),
-            dma((2,)), dma((2, 2 * regions)), dma((2, 8 * hids)), dma((2, 1)),
+            low(hids, 2 * latent, width),
+            dma((2,)), dma((2, 2 * regions)), dma((2, 9 * hids)), dma((2, 1)),
             dma((2, 3 * regions)), dma((2, 3 * regions)),
         ],
         compiler_params=pltpu.CompilerParams(
@@ -466,7 +469,7 @@
         ),
     )(
         agg, node_lat, cotangent, norm_gain[None], w_edge_in[latent:], edge_lat, slope,
-        send_rows, cell, *weo, *wni, *bn, *wno,
+        send_rows, cell, *weo, w_node_in, *bn, *wno,
     )
 
 

time: 110 us -> 99.6 us (0.905)
  waiting for transfers between devices: 11.2 us -> 0.2 us
    ppermute x4 -> x3, waiting for transfers between devices: 11.2 us -> 0.2 us  [hid_shift(): lax.ppermute(value, 'hid', [(i, (i + by) % hids) for i in range(hids)])]
    ppermute x4 -> x3, starting transfers between devices: 2.96 us -> 2.69 us  [hid_shift(): lax.ppermute(value, 'hid', [(i, (i + by) % hids) for i in range(hids)])]
  transfers between devices with their start and end apart: 5 -> 4, of which waited for: 1 -> 1; matrix products, arithmetic and copies ran while one was open for 6% -> 6% of each run, Pallas kernels for 4% -> 5%
where the time goes in v3:
time: 99.6 us; the launch traced here: 97.8 us
  Pallas kernels  78.7 us (79%)
  local copies, waits for them, and re-layouts  11.8 us (12%)
  starting transfers between devices  3.71 us (4%)
  other arithmetic  1.43 us (1%)
  matrix products  1.25 us (1%)
    pallas_call x1, Pallas kernels, on_device(): pl.pallas_call(functools.partial(core_kernel, regions, hids, blocks, per_...  74.2 us
    unnamed x22, local copies, waits for them, and re-layouts  7.76 us
    pallas_call x1, Pallas kernels, on_device(): pl.pallas_call(functools.partial(edge_forward_kernel, block_rows, per_ste...  4.46 us
    ppermute x3, starting transfers between devices, hid_shift(): lax.ppermute(value, 'hid', [(i, (i + by) % hids) for i in range(hids)])  2.69 us
  transfers between devices with their start and end apart: 4, of which 1 were waited for; matrix products, arithmetic and copies ran while one was open for 6% of the time, Pallas kernels for 5%

profile of v3, /device:TPU:25, one launch (start us, length us, event | category | flops | bytes accessed | tf_op | source)
XLA Modules:
  0.0 97.8 jit_solution(11454391658102771670)
XLA Ops:
  0.6 0.0 copy-start.2
  0.6 0.0 copy-start.5
  0.7 0.0 copy-start.6
  0.7 0.0 copy-start.4
  0.7 0.0 copy-start.3
  0.7 0.8 broadcast_in_dim.12.refs_12_
  1.5 1.2 %collective-permute-start.2 = (bf16[1,256]{1,0:T(2,128)(2,1)S(1)}, bf16[1,256]{1,0:T(2,128)(2,1)S(1)}, u32[]{:S(2)}, u32[]{:S(2)}) collective-permute-start(bf16[1,256]{1,0:T(2,128)(2,1)S(1)} %broadcast_in_dim.12.refs_12_), channel_id=1, source_target_pairs={{0,2},{2,0},{1,3},{3,1},{4,6},{6,4},{5,7},{7,5},{8,10},{10,8},{9,1... | collective-permute-start | bytes 1544 | tf_op jit(solution)/shard_map/ppermute | solution.py:379
  2.7 1.3 %convolution_convert_fusion.own_part = bf16[256,256]{1,0:T(8,128)(2,1)S(1)} fusion(bf16[256,512]{1,0:T(8,128)(2,1)} %refs_1_.1, bf16[1024,256]{1,0:T(8,128)(2,1)} %param.20), kind=kOutput, calls=%fused_computation | convolution fusion | flops 67174400 | bytes 655360 | tf_op jit(solution)/shard_map/dot_general | solution.py:388
  3.9 1.0 %collective-permute-start = (bf16[256,256]{1,0:T(8,128)(2,1)S(1)}, bf16[256,256]{1,0:T(8,128)(2,1)S(1)}, u32[]{:S(2)}, u32[]{:S(2)}) collective-permute-start(bf16[256,256]{1,0:T(8,128)(2,1)S(1)} %convolution_convert_fusion.own_part), channel_id=1, source_target_pairs={{0,1},{1,0},{2,3},{3,2},{4,5},{5,4},{6,7},{7,6},{8,9},{9,8},{10,11... | collective-permute-start | bytes 393224 | tf_op jit(solution)/shard_map/ppermute | solution.py:376
  4.9 0.3 collective-permute-start.1
  5.2 1.2 %collective-permute-start.3 = (bf16[256,512]{1,0:T(8,128)(2,1)}, bf16[256,512]{1,0:T(8,128)(2,1)S(1)}, u32[]{:S(2)}, u32[]{:S(2)}) collective-permute-start(bf16[256,512]{1,0:T(8,128)(2,1)} %refs_14_.1), channel_id=1, source_target_pairs={{0,2},{2,0},{1,3},{3,1},{4,6},{6,4},{5,7},{7,5},{8,10},{10,8},{9,1... | collective-permute-start | bytes 786440 | tf_op jit(solution)/shard_map/ppermute | solution.py:379
  6.4 1.1 %fusion.15 = (bf16[512,256]{1,0:T(8,128)(2,1)S(1)}, bf16[512,256]{1,0:T(8,128)(2,1)S(1)}) fusion(bf16[1024,256]{1,0:T(8,128)(2,1)} %param.20), kind=kLoop, calls=%fused_computation.26 | loop fusion | bytes 1048576 | tf_op jit(solution)/shard_map/slice | solution.py:388
  7.5 0.7 fusion.13
  8.2 0.7 broadcast_in_dim.10.bias
  8.8 0.7 broadcast_in_dim.11.refs_3_
  9.5 0.1 add.55
  9.6 0.7 fusion.2
  10.3 0.7 reshape.58.slot
  11.1 0.1 add.56
  11.2 0.0 collective-permute-done.other_part
  11.2 0.0 copy-start
  11.2 1.7 %copy-done = bf16[2560,512]{1,0:T(8,128)(2,1)S(1)} copy-done((bf16[2560,512]{1,0:T(8,128)(2,1)S(1)}, bf16[2560,512]{1,0:T(8,128)(2,1)}, u32[]{:S(2)}) %copy-start) | copy-done | bytes 2621464
  12.9 4.5 %shard_map.181 = (bf16[1024,256]{1,0:T(8,128)(2,1)S(1)}, bf16[2560,256]{1,0:T(8,128)(2,1)S(1)}) custom-call(s32[20]{0:T(128)S(1)} %get-tuple-element.13.codes, bf16[2560,512]{1,0:T(8,128)(2,1)S(1)} %copy-done, s32[5,1,512]{2,1,0:T(1,128)S(1)} %reshape.57.send.refs_7_, s32[5,1,512]{2,1,0:T(1,128)S(1)} %reshape.58.slot, ...), custom_call_target="tpu_custom_call" | custom-call | tf_op jit(solution)/shard_map/pallas_call | solution.py:405
  17.4 0.0 copy-start.1
  17.4 1.1 %copy-done.1 = bf16[2560,256]{1,0:T(8,128)(2,1)} copy-done((bf16[2560,256]{1,0:T(8,128)(2,1)}, bf16[2560,256]{1,0:T(8,128)(2,1)S(1)}, u32[]{:S(2)}) %copy-start.1) | copy-done | bytes 1310744
  18.5 0.0 collective-permute-done.2.refs_13_
  18.5 0.0 collective-permute-done.1.refs_10_
  18.5 0.2 collective-permute-done.3.refs_15_
  18.7 0.0 copy-done.2
  18.7 0.0 copy-done.5
  18.7 0.0 copy-done.6
  18.7 0.0 copy-done.4
  18.7 0.0 copy-done.3
  18.7 74.2 %shard_map.182 = (bf16[256,512]{1,0:T(8,128)(2,1)S(1)}, bf16[256,512]{1,0:T(8,128)(2,1)S(1)}, f32[1024,256]{1,0:T(8,128)S(1)}, f32[256,512]{1,0:T(8,128)S(1)}, f...) custom-call(bf16[4,256,256]{2,1,0:T(8,128)(2,1)S(1)} %bitcast.9, bf16[256,512]{1,0:T(8,128)(2,1)S(1)} %copy-done.2, ...), custom_call_target="tpu_custom_call" | custom-call | tf_op jit(solution)/shard_map/pallas_call | solution.py:439
  92.9 0.0 copy-start.7
  92.9 0.7 copy.26
  93.6 0.7 copy.27
  94.3 1.0 copy.28
  95.3 0.8 copy.29
  96.1 0.0 copy-done.7
  96.1 1.0 copy.30
  97.1 0.8 copy.31
  (2 shorter events, 0.0 us)
Async XLA Ops:
  0.6 18.0 %copy-start.2 = (bf16[256,512]{1,0:T(8,128)(2,1)S(1)}, bf16[256,512]{1,0:T(8,128)(2,1)}, u32[]{:S(2)}) copy-start(bf16[256,512]{1,0:T(8,128)(2,1)} %refs_1_.1) | copy-start | bytes 786436
  0.6 18.0 %copy-start.5 = (bf16[256,512]{1,0:T(8,128)(2,1)S(1)}, bf16[256,512]{1,0:T(8,128)(2,1)}, u32[]{:S(2)}) copy-start(bf16[256,512]{1,0:T(8,128)(2,1)} %refs_9_.1) | copy-start | bytes 786436
  0.7 18.0 %copy-start.6 = (bf16[256,512]{1,0:T(8,128)(2,1)S(1)}, bf16[256,512]{1,0:T(8,128)(2,1)}, u32[]{:S(2)}) copy-start(bf16[256,512]{1,0:T(8,128)(2,1)} %refs_14_.1) | copy-start | bytes 786436
  0.7 18.0 %copy-start.4 = (bf16[256,512]{1,0:T(8,128)(2,1)S(1)}, bf16[256,512]{1,0:T(8,128)(2,1)}, u32[]{:S(2)}) copy-start(bf16[256,512]{1,0:T(8,128)(2,1)} %refs_2_.1) | copy-start | bytes 786436
  0.7 18.0 %copy-start.3 = (bf16[1024,256]{1,0:T(8,128)(2,1)S(1)}, bf16[1024,256]{1,0:T(8,128)(2,1)}, u32[]{:S(2)}) copy-start(bf16[1024,256]{1,0:T(8,128)(2,1)} %refs_11_.1) | copy-start | bytes 1572868
  1.5 17.0 %collective-permute-start.2 = (bf16[1,256]{1,0:T(2,128)(2,1)S(1)}, bf16[1,256]{1,0:T(2,128)(2,1)S(1)}, u32[]{:S(2)}, u32[]{:S(2)}) collective-permute-start(bf16[1,256]{1,0:T(2,128)(2,1)S(1)} %broadcast_in_dim.12.refs_12_), channel_id=1, source_target_pairs={{0,2},{2,0},{1,3},{3,1},{4,6},{6,4},{5,7},{7,5},{8,10},{10,8},{9,1... | collective-permute-start | bytes 1544 | tf_op jit(solution)/shard_map/ppermute | solution.py:379
  3.9 7.2 %collective-permute-start = (bf16[256,256]{1,0:T(8,128)(2,1)S(1)}, bf16[256,256]{1,0:T(8,128)(2,1)S(1)}, u32[]{:S(2)}, u32[]{:S(2)}) collective-permute-start(bf16[256,256]{1,0:T(8,128)(2,1)S(1)} %convolution_convert_fusion.own_part), channel_id=1, source_target_pairs={{0,1},{1,0},{2,3},{3,2},{4,5},{5,4},{6,7},{7,6},{8,9},{9,8},{10,11... | collective-permute-start | bytes 393224 | tf_op jit(solution)/shard_map/ppermute | solution.py:376
  4.9 13.5 %collective-permute-start.1 = (bf16[256,512]{1,0:T(8,128)(2,1)}, bf16[256,512]{1,0:T(8,128)(2,1)S(1)}, u32[]{:S(2)}, u32[]{:S(2)}) collective-permute-start(bf16[256,512]{1,0:T(8,128)(2,1)} %refs_9_.1), channel_id=1, source_target_pairs={{0,2},{2,0},{1,3},{3,1},{4,6},{6,4},{5,7},{7,5},{8,10},{10,8},{9,1... | collective-permute-start | bytes 786440 | tf_op jit(solution)/shard_map/ppermute | solution.py:379
  5.2 13.4 %collective-permute-start.3 = (bf16[256,512]{1,0:T(8,128)(2,1)}, bf16[256,512]{1,0:T(8,128)(2,1)S(1)}, u32[]{:S(2)}, u32[]{:S(2)}) collective-permute-start(bf16[256,512]{1,0:T(8,128)(2,1)} %refs_14_.1), channel_id=1, source_target_pairs={{0,2},{2,0},{1,3},{3,1},{4,6},{6,4},{5,7},{7,5},{8,10},{10,8},{9,1... | collective-permute-start | bytes 786440 | tf_op jit(solution)/shard_map/ppermute | solution.py:379
  11.2 1.7 %copy-start = (bf16[2560,512]{1,0:T(8,128)(2,1)S(1)}, bf16[2560,512]{1,0:T(8,128)(2,1)}, u32[]{:S(2)}) copy-start(bf16[2560,512]{1,0:T(8,128)(2,1)} %refs_5_.1) | copy-start | bytes 7864324
  17.4 1.1 %copy-start.1 = (bf16[2560,256]{1,0:T(8,128)(2,1)}, bf16[2560,256]{1,0:T(8,128)(2,1)S(1)}, u32[]{:S(2)}) copy-start(bf16[2560,256]{1,0:T(8,128)(2,1)S(1)} %get-tuple-element.9.refs_6_) | copy-start | bytes 3932164
  92.9 3.2 %copy-start.7 = (f32[1024,256]{1,0:T(8,128)S(1)}, f32[1024,256]{1,0:T(8,128)}, u32[]{:S(2)}) copy-start(f32[1024,256]{1,0:T(8,128)} %get-tuple-element.24) | copy-start | bytes 3145732
